TPU v7x, 32 devices: a whole 2x2x4 slice. The times are simulated.
32 devices in a mesh: fsdp: 32 (over z, y, x, core).
Axes of the slice: x: 2, y: 2, z: 4, core: 2. Of those that a mesh axis runs over, the one named last changes fastest.
Arguments:
- tokens: bfloat16 [8192, 2048], P('fsdp'), may hold values from -6 to 6
- cotangent: bfloat16 [8192, 2048], P('fsdp'), may hold values from -6 to 6
- lengths: int32 [4], replicated, may hold values from 1024 to 4096, as said below
- attend_in: float32 [2048, 6144], P('fsdp'), may hold values from -0.125 to 0.125
- widening: float32 [2048, 8192], P('fsdp'), may hold values from -0.125 to 0.125
- attend_out: float32 [2048, 2048], P('fsdp'), may hold values from -2.5 to 2.5
- narrowing: float32 [2048, 8192], P('fsdp'), may hold values from -0.0625 to 0.0625
- small_params: float32 [2048, 13], P('fsdp'), as said below
- first_attend_in: float32 [2048, 6144], P('fsdp'), may hold values from -64 to 64
- first_widening: float32 [2048, 8192], P('fsdp'), may hold values from -20 to 20
- first_attend_out: float32 [2048, 2048], P('fsdp'), may hold values from -4 to 4
- first_narrowing: float32 [2048, 8192], P('fsdp'), may hold values from -32 to 32
- first_small: float32 [2048, 13], P('fsdp'), may hold values from -64 to 64
- second_attend_in: float32 [2048, 6144], P('fsdp'), may hold values from 434.176 to 1720.32
- second_widening: float32 [2048, 8192], P('fsdp'), may hold values from 53.248 to 212.992
- second_attend_out: float32 [2048, 2048], P('fsdp'), may hold values from 1 to 4
- second_narrowing: float32 [2048, 8192], P('fsdp'), may hold values from 155.648 to 622.592
- second_small: float32 [2048, 13], P('fsdp'), may hold values from 434.176 to 1720.32
Outputs:
- block_out: bfloat16 [8192, 2048], P('fsdp')
- token_grad: float32 [8192, 2048], P('fsdp')
- new_attend_in: float32 [2048, 6144], P('fsdp')
- new_widening: float32 [2048, 8192], P('fsdp')
- new_attend_out: float32 [2048, 2048], P('fsdp')
- new_narrowing: float32 [2048, 8192], P('fsdp')
- new_small: float32 [2048, 13], P('fsdp')
- mean_attend_in: float32 [2048, 6144], P('fsdp')
- mean_widening: float32 [2048, 8192], P('fsdp')
- mean_attend_out: float32 [2048, 2048], P('fsdp')
- mean_narrowing: float32 [2048, 8192], P('fsdp')
- mean_small: float32 [2048, 13], P('fsdp')
- square_attend_in: float32 [2048, 6144], P('fsdp')
- square_widening: float32 [2048, 8192], P('fsdp')
- square_attend_out: float32 [2048, 2048], P('fsdp')
- square_narrowing: float32 [2048, 8192], P('fsdp')
- square_small: float32 [2048, 13], P('fsdp')
Inputs may be any that keep to these rules, and one draw needn't show every extreme that they name: The 4 lengths sum to 8192; each is 1024 or more and one is exactly 4096. `small_params`: gains near one in columns 0 and 2, biases of a tenth elsewhere.
All inputs are finite; a program needn't handle non-finite values.
Results may differ from a plain program's by a relative error of at most 0.011.
Values may be sent and summed in bfloat16 or wider, within the bound.
A program may use at most 704 MiB of HBM per device.

v0:
```python
from functools import partial

import jax
import jax.numpy as jnp
from jax import lax
from jax.sharding import PartitionSpec as P

D = 2048
HEADS = 8
FF = 8192
LMAX = 4096
STEPS = 10


NORM_EPS = 1e-05
ADAM_EPS = 1e-08
BETA_ONE = 0.9
BETA_TWO = 0.95
WEIGHT_DECAY = 0.01
NEGATIVE = -1e30
ROPE_BASE = 10000.0


def shifted(value, axis, by):
    peers = lax.axis_size(axis)
    pairs = [(i, i + by) for i in range(peers) if 0 <= i + by < peers]
    return lax.ppermute(value, axis, pairs)


def layer_norm(values, gain_vector, shift_vector):
    average = jnp.mean(values, axis=-1, keepdims=True)
    centred = values - average
    spread = jnp.mean(centred * centred, axis=-1, keepdims=True)
    return centred * lax.rsqrt(spread + NORM_EPS) * gain_vector + shift_vector


def token_places(global_rows, lengths):
    seq_ends = jnp.cumsum(lengths)
    starts = seq_ends - lengths
    member = (global_rows[:, None] >= starts[None, :]) & (global_rows[:, None] < seq_ends[None, :])
    numbers = jnp.arange(lengths.shape[0], dtype=jnp.int32)
    seq_ids = jnp.sum(jnp.where(member, numbers[None, :], 0), axis=1)
    offsets = global_rows - jnp.sum(jnp.where(member, starts[None, :], 0), axis=1)
    return (seq_ids, offsets, jnp.any(member, axis=1))


def rotate(values, offsets):
    rotary = values.shape[-1] // 4
    half_rotary = rotary // 2
    frequency = ROPE_BASE ** (-2.0 * jnp.arange(half_rotary, dtype=jnp.float32) / rotary)
    angles = offsets.astype(jnp.float32)[:, None] * frequency[None, :]
    cosine = jnp.cos(angles)[:, None, :]
    sine_part = jnp.sin(angles)[:, None, :]
    first_half = values[..., :half_rotary]
    second_half = values[..., half_rotary:rotary]
    return jnp.concatenate(
        [
            first_half * cosine - second_half * sine_part,
            second_half * cosine + first_half * sine_part,
            values[..., rotary:],
        ],
        axis=-1,
    )


def adam_step(parameter, gradient, first_moment, second_moment, step_rate):
    first_new = BETA_ONE * first_moment + (1.0 - BETA_ONE) * gradient
    second_new = BETA_TWO * second_moment + (1.0 - BETA_TWO) * gradient * gradient
    first_hat = first_new / (1.0 - BETA_ONE**STEPS)
    second_hat = second_new / (1.0 - BETA_TWO**STEPS)
    parameter_new = parameter - step_rate * (
        first_hat / (jnp.sqrt(second_hat) + ADAM_EPS) + WEIGHT_DECAY * parameter
    )
    return (first_new, second_new, parameter_new)


def contract_rows(left, right):
    return lax.dot_general(
        left, right, (((0,), (0,)), ((), ())), preferred_element_type=jnp.float32
    )


def contract_cols(left, right):
    return lax.dot_general(
        left, right, (((1,), (1,)), ((), ())), preferred_element_type=jnp.float32
    )


def body(
    tokens,
    cotangent,
    lengths,
    attend_in,
    widening,
    attend_out,
    narrowing,
    small_params,
    first_attend_in,
    first_widening,
    first_attend_out,
    first_narrowing,
    first_small,
    second_attend_in,
    second_widening,
    second_attend_out,
    second_narrowing,
    second_small,
):
    tok_rows = tokens.shape[0]
    device = lax.axis_index("fsdp")
    all_small = lax.all_gather(small_params, "fsdp", axis=0, tiled=True)
    model_width = all_small.shape[0]
    hidden_width = widening.shape[1]
    head_count = HEADS
    head_size = model_width // head_count
    score_scale = head_size ** (-0.5)
    back_blocks = LMAX // tok_rows
    window_rows = (back_blocks + 1) * tok_rows
    query_pos = device * tok_rows + jnp.arange(tok_rows, dtype=jnp.int32)
    key_pos = (device - back_blocks) * tok_rows + jnp.arange(window_rows, dtype=jnp.int32)
    query_ids, offsets, unused_valid = token_places(query_pos, lengths)
    key_ids, unused_offsets, key_valid = token_places(key_pos, lengths)
    visible = (
        (key_pos[None, :] <= query_pos[:, None])
        & (key_ids[None, :] == query_ids[:, None])
        & key_valid[None, :]
    )
    resid = tokens.astype(jnp.float32)

    def both_norms(resid_in, small_in):
        return (
            layer_norm(resid_in, small_in[:, 0], small_in[:, 1]),
            layer_norm(resid_in, small_in[:, 2], small_in[:, 3]),
        )

    (norm_one, norm_two), norm_pull = jax.vjp(both_norms, resid, all_small)
    input_one = norm_one.astype(jnp.bfloat16)
    input_two = norm_two.astype(jnp.bfloat16)
    bias_joint = all_small[:, 4:7].T.reshape(-1)
    bias_up = all_small[:, 9:].reshape(-1)
    inner_low = attend_in.astype(jnp.bfloat16)
    wide_low = widening.astype(jnp.bfloat16)
    outer_low = attend_out.astype(jnp.bfloat16)
    narrow_low = narrowing.astype(jnp.bfloat16)
    pieces = (
        lax.all_gather(inner_low, "fsdp", axis=0, tiled=True),
        lax.all_gather(wide_low, "fsdp", axis=0, tiled=True),
    )
    cols_one = input_one
    cols_two = input_two
    joint_sum = jnp.dot(cols_one, pieces[0], preferred_element_type=jnp.float32)
    hidden_sum = jnp.dot(cols_two, pieces[1], preferred_element_type=jnp.float32)
    joint = joint_sum + bias_joint
    hidden = hidden_sum + bias_up

    def rope_pair(query_lin, key_lin):
        query_rot = rotate(query_lin.reshape(tok_rows, head_count, head_size), offsets)
        key_rot = rotate(key_lin.reshape(tok_rows, head_count, head_size), offsets)
        return (query_rot.reshape(tok_rows, model_width), key_rot.reshape(tok_rows, model_width))

    (query_rot, key_rot), rope_pull = jax.vjp(
        rope_pair, joint[:, :model_width], joint[:, model_width : 2 * model_width]
    )
    queries_low = query_rot.astype(jnp.bfloat16)
    keys_low = key_rot.astype(jnp.bfloat16)
    values_low = joint[:, 2 * model_width :].astype(jnp.bfloat16)
    pair_low = jnp.stack([keys_low, values_low])

    def fetch_step(moving, unused_item):
        arrived = shifted(moving, "fsdp", 1)
        return (arrived, (arrived[0], arrived[1]))

    unused_last, (earlier_keys, earlier_values) = lax.scan(
        fetch_step, pair_low, None, length=back_blocks
    )
    window_keys = jnp.concatenate([earlier_keys[::-1], keys_low[None]], 0)
    window_values = jnp.concatenate([earlier_values[::-1], values_low[None]], 0)

    def head_forward(head_index):
        first_col = head_index * head_size
        query_head = lax.dynamic_slice_in_dim(queries_low, first_col, head_size, 1)
        key_head = lax.dynamic_slice_in_dim(window_keys, first_col, head_size, 2).reshape(
            window_rows, head_size
        )
        value_head = lax.dynamic_slice_in_dim(window_values, first_col, head_size, 2).reshape(
            window_rows, head_size
        )
        scores = jnp.where(visible, contract_cols(query_head, key_head) * score_scale, NEGATIVE)
        row_top = jnp.max(scores, axis=-1, keepdims=True)
        log_total = jnp.log(jnp.sum(jnp.exp(scores - row_top), axis=-1, keepdims=True)) + row_top
        soft_weights = jnp.exp(scores - log_total).astype(jnp.bfloat16)
        return (
            jnp.dot(soft_weights, value_head, preferred_element_type=jnp.float32),
            log_total[:, 0],
        )

    head_out, head_totals = lax.map(head_forward, jnp.arange(head_count, dtype=jnp.int32))
    attended = head_out.transpose(1, 0, 2).reshape(tok_rows, model_width).astype(jnp.bfloat16)
    gelu_values, gelu_pull = jax.vjp(partial(jax.nn.gelu, approximate=False), hidden)
    activated = gelu_values.astype(jnp.bfloat16)
    pieces = (
        lax.all_gather(outer_low, "fsdp", axis=0, tiled=True),
        lax.all_gather(narrow_low, "fsdp", axis=0, tiled=True),
    )
    term = contract_cols(attended, pieces[0]) + contract_cols(activated, pieces[1])
    branches = lax.dynamic_update_slice_in_dim(
        jnp.zeros((tok_rows, model_width), jnp.float32), term, jnp.int32(0), 1
    )
    block_out = (resid + branches + all_small[:, 7] + all_small[:, 8]).astype(jnp.bfloat16)
    pieces = (
        lax.all_gather(outer_low, "fsdp", axis=0, tiled=True),
        lax.all_gather(narrow_low, "fsdp", axis=0, tiled=True),
    )
    cols_out = cotangent
    grad_attended = jnp.dot(cols_out, pieces[0], preferred_element_type=jnp.float32)
    grad_activated = jnp.dot(cols_out, pieces[1], preferred_element_type=jnp.float32)
    grad_att_low = grad_attended.astype(jnp.bfloat16)
    grad_hidden = gelu_pull(grad_activated)[0].astype(jnp.bfloat16)

    def refetch_step(moving, unused_item):
        arrived = shifted(moving, "fsdp", 1)
        return (arrived, (arrived[0], arrived[1]))

    unused_again, (again_keys, again_values) = lax.scan(
        refetch_step, pair_low, None, length=back_blocks
    )
    keys_back = jnp.concatenate([again_keys[::-1], keys_low[None]], 0)
    values_back = jnp.concatenate([again_values[::-1], values_low[None]], 0)
    queries_grid = queries_low.reshape(tok_rows, head_count, head_size)
    grads_grid = grad_att_low.reshape(tok_rows, head_count, head_size)
    deltas = jnp.sum(head_out * grads_grid.transpose(1, 0, 2).astype(jnp.float32), axis=-1)

    def block_grads(block_index):
        key_grid = lax.dynamic_index_in_dim(keys_back, block_index, 0, keepdims=False).reshape(
            tok_rows, head_count, head_size
        )
        value_grid = lax.dynamic_index_in_dim(values_back, block_index, 0, keepdims=False).reshape(
            tok_rows, head_count, head_size
        )
        seen = lax.dynamic_slice_in_dim(visible, block_index * tok_rows, tok_rows, 1)
        scores = (
            jnp.einsum("qhd,khd->hqk", queries_grid, key_grid, preferred_element_type=jnp.float32)
            * score_scale
        )
        scores = jnp.where(seen[None], scores, NEGATIVE)
        soft_weights = jnp.exp(scores - head_totals[:, :, None])
        grad_soft = jnp.einsum(
            "qhd,khd->hqk", grads_grid, value_grid, preferred_element_type=jnp.float32
        )
        grad_scores = (soft_weights * (grad_soft - deltas[:, :, None])).astype(jnp.bfloat16)
        grad_query = (
            jnp.einsum("hqk,khd->qhd", grad_scores, key_grid, preferred_element_type=jnp.float32)
            * score_scale
        )
        grad_key = (
            jnp.einsum(
                "hqk,qhd->khd", grad_scores, queries_grid, preferred_element_type=jnp.float32
            )
            * score_scale
        )
        grad_value = jnp.einsum(
            "hqk,qhd->khd",
            soft_weights.astype(jnp.bfloat16),
            grads_grid,
            preferred_element_type=jnp.float32,
        )
        return (
            grad_query.reshape(tok_rows, model_width),
            jnp.stack(
                [grad_key.reshape(tok_rows, model_width), grad_value.reshape(tok_rows, model_width)]
            ),
        )

    query_start, key_start = block_grads(0)

    def return_step(state, block_index):
        query_total, moving = state
        arrived = shifted(moving.astype(jnp.bfloat16), "fsdp", -1).astype(moving.dtype)
        query_part, key_part = block_grads(block_index)
        return ((query_total + query_part, arrived + key_part), None)

    (query_sum, own_pair), unused_steps = lax.scan(
        return_step, (query_start, key_start), jnp.arange(1, back_blocks + 1, dtype=jnp.int32)
    )
    grad_query_lin, grad_key_lin = rope_pull((query_sum, own_pair[0]))
    grad_joint = jnp.concatenate([grad_query_lin, grad_key_lin, own_pair[1]], 1).astype(
        jnp.bfloat16
    )
    pieces = (
        lax.all_gather(inner_low, "fsdp", axis=0, tiled=True),
        lax.all_gather(wide_low, "fsdp", axis=0, tiled=True),
    )
    term_one = contract_cols(grad_joint, pieces[0])
    term_two = contract_cols(grad_hidden, pieces[1])
    grad_resid, grad_small_norm = norm_pull((term_one, term_two))
    token_grad = cotangent.astype(jnp.float32) + grad_resid
    joint_bias_grad = jnp.sum(grad_joint.astype(jnp.float32), axis=0).reshape(3, model_width).T
    out_bias_grad = jnp.sum(cotangent.astype(jnp.float32), axis=0)[:, None]
    up_bias_grad = jnp.sum(grad_hidden.astype(jnp.float32), axis=0).reshape(
        model_width, hidden_width // model_width
    )
    small_term = jnp.concatenate(
        [grad_small_norm[:, :4], joint_bias_grad, out_bias_grad, out_bias_grad, up_bias_grad], 1
    )
    small_grad = lax.psum_scatter(small_term, "fsdp", scatter_dimension=0, tiled=True)
    cols_one = input_one
    cols_two = input_two
    cols_out = cotangent
    owned = lax.psum_scatter(
        jnp.concatenate(
            [
                contract_rows(cols_one, grad_joint),
                contract_rows(cols_two, grad_hidden),
                contract_rows(cols_out, attended),
                contract_rows(cols_out, activated),
            ],
            1,
        ),
        "fsdp",
        scatter_dimension=0,
        tiled=True,
    )
    grad_inner = owned[:, : 3 * model_width]
    grad_wide = owned[:, 3 * model_width : 3 * model_width + hidden_width]
    grad_outer = owned[:, 3 * model_width + hidden_width : 4 * model_width + hidden_width]
    grad_narrow = owned[:, 4 * model_width + hidden_width :]
    rate_inner = 2.5 * D ** (-0.5)
    rate_outer = 2.5 * (D * 11 // LMAX) ** (-0.5)
    rate_down = 2.5 * FF ** (-0.5)
    rate_small = 0.5
    mean_in, square_in, new_in = adam_step(
        attend_in, grad_inner, first_attend_in, second_attend_in, rate_inner
    )
    mean_wide, square_wide, new_wide = adam_step(
        widening, grad_wide, first_widening, second_widening, rate_inner
    )
    mean_out, square_out, new_out = adam_step(
        attend_out, grad_outer, first_attend_out, second_attend_out, rate_outer
    )
    mean_narrow, square_narrow, new_narrow = adam_step(
        narrowing, grad_narrow, first_narrowing, second_narrowing, rate_down
    )
    mean_small, square_small, new_small = adam_step(
        small_params, small_grad, first_small, second_small, rate_small
    )
    return (
        block_out,
        token_grad,
        new_in,
        new_wide,
        new_out,
        new_narrow,
        new_small,
        mean_in,
        mean_wide,
        mean_out,
        mean_narrow,
        mean_small,
        square_in,
        square_wide,
        square_out,
        square_narrow,
        square_small,
    )


def solution(mesh):
    return jax.shard_map(
        body,
        mesh=mesh,
        in_specs=(
            P("fsdp", None),
            P("fsdp", None),
            P(),
            P("fsdp", None),
            P("fsdp", None),
            P("fsdp", None),
            P("fsdp", None),
            P("fsdp", None),
            P("fsdp", None),
            P("fsdp", None),
            P("fsdp", None),
            P("fsdp", None),
            P("fsdp", None),
            P("fsdp", None),
            P("fsdp", None),
            P("fsdp", None),
            P("fsdp", None),
            P("fsdp", None),
        ),
        out_specs=(
            P("fsdp", None),
            P("fsdp", None),
            P("fsdp", None),
            P("fsdp", None),
            P("fsdp", None),
            P("fsdp", None),
            P("fsdp", None),
            P("fsdp", None),
            P("fsdp", None),
            P("fsdp", None),
            P("fsdp", None),
            P("fsdp", None),
            P("fsdp", None),
            P("fsdp", None),
            P("fsdp", None),
            P("fsdp", None),
            P("fsdp", None),
        ),
        check_vma=False,
    )
```

profile of v0, /device:TPU:0, one launch (start us, length us, event | category | flops | bytes accessed | tf_op | source)
XLA Modules:
  0.0 3797.7 jit_solution(13829591026808368646)
XLA Ops:
  16.3 44.6 %all-gather = f32[32,64,13]{1,2,0:T(8,128)S(1)} all-gather(f32[1,64,13]{1,2,0:T(8,128)S(1)} %bitcast.238), channel_id=1, replica_groups=mesh['fsdp'=32] {'fsdp'}, dimensions={0}, use_global_device_ids=true | all-gather | bytes 109824 | tf_op jit(solution)/shard_map/all_gather | solution.py:111
  100.9 148.1 %all-gather.6.cloned.1.call-done = bf16[2048,6144]{1,0:T(8,128)(2,1)} async-done(((bf16[64,6144]{1,0:T(8,128)(2,1)}), bf16[2048,6144]{1,0:T(8,128)(2,1)}) %all-gather.6.cloned.1.call-update) | async-done | bytes 25165840 | tf_op jit(solution)/shard_map/all_gather | solution.py:146
  277.1 637.4 %while.45 = (s32[]{:T(128)}, bf16[2,256,2048]{2,1,0:T(8,128)(2,1)}, bf16[16,256,2048]{2,1,0:T(8,128)(2,1)}, bf16[16,256,2048]{2,1,0:T(8,128)(2,1)}, s32[]{:T(128)}) while((s32[]{:T(128)}, bf16[2,256,2048]{2,1,0:T(8,128)(2,1)}, bf16[16,256,2048]{2,1,0:T(8,128)(2,1)}, bf16[16,256,2048]{2,1,0:T(8,128)(2,1)}, s32[]{:T(128)}) %tuple.120), condition=%wide.region_5.6_spmd, body=%wide.region_4.5_spmd.sunk | while | flops 2 | bytes 16777328 | solution.py:173
  286.0 45.2 %collective-permute-start = (bf16[2,256,2048]{2,1,0:T(8,128)(2,1)}, bf16[2,256,2048]{2,1,0:T(8,128)(2,1)S(1)}, u32[]{:S(2)}, u32[]{:S(2)}) collective-permute-start(bf16[2,256,2048]{2,1,0:T(8,128)(2,1)} %get-tuple-element.627), channel_id=1, source_target_pairs={{0,1},{1,2},{2,3},{3,4},{4,5},{5,6},{6,7},{7,8},{8,9},{9,10},{10,1... | collective-permute-start | bytes 6291464 | tf_op jit(solution)/shard_map/while/body/eval_jaxpr/ppermute | solution.py:27
  371.2 65.6 %collective-permute-start = (bf16[2,256,2048]{2,1,0:T(8,128)(2,1)}, bf16[2,256,2048]{2,1,0:T(8,128)(2,1)S(1)}, u32[]{:S(2)}, u32[]{:S(2)}) collective-permute-start(bf16[2,256,2048]{2,1,0:T(8,128)(2,1)} %get-tuple-element.627), channel_id=1, source_target_pairs={{0,1},{1,2},{2,3},{3,4},{4,5},{5,6},{6,7},{7,8},{8,9},{9,10},{10,1... | collective-permute-start | bytes 6291464 | tf_op jit(solution)/shard_map/while/body/eval_jaxpr/ppermute | solution.py:27
  443.5 27.5 collective-permute-start
  477.6 23.7 collective-permute-start
  507.9 31.2 collective-permute-start
  545.8 53.6 %collective-permute-start = (bf16[2,256,2048]{2,1,0:T(8,128)(2,1)}, bf16[2,256,2048]{2,1,0:T(8,128)(2,1)S(1)}, u32[]{:S(2)}, u32[]{:S(2)}) collective-permute-start(bf16[2,256,2048]{2,1,0:T(8,128)(2,1)} %get-tuple-element.627), channel_id=1, source_target_pairs={{0,1},{1,2},{2,3},{3,4},{4,5},{5,6},{6,7},{7,8},{8,9},{9,10},{10,1... | collective-permute-start | bytes 6291464 | tf_op jit(solution)/shard_map/while/body/eval_jaxpr/ppermute | solution.py:27
  606.1 49.2 %collective-permute-start = (bf16[2,256,2048]{2,1,0:T(8,128)(2,1)}, bf16[2,256,2048]{2,1,0:T(8,128)(2,1)S(1)}, u32[]{:S(2)}, u32[]{:S(2)}) collective-permute-start(bf16[2,256,2048]{2,1,0:T(8,128)(2,1)} %get-tuple-element.627), channel_id=1, source_target_pairs={{0,1},{1,2},{2,3},{3,4},{4,5},{5,6},{6,7},{7,8},{8,9},{9,10},{10,1... | collective-permute-start | bytes 6291464 | tf_op jit(solution)/shard_map/while/body/eval_jaxpr/ppermute | solution.py:27
  661.9 50.2 %collective-permute-start = (bf16[2,256,2048]{2,1,0:T(8,128)(2,1)}, bf16[2,256,2048]{2,1,0:T(8,128)(2,1)S(1)}, u32[]{:S(2)}, u32[]{:S(2)}) collective-permute-start(bf16[2,256,2048]{2,1,0:T(8,128)(2,1)} %get-tuple-element.627), channel_id=1, source_target_pairs={{0,1},{1,2},{2,3},{3,4},{4,5},{5,6},{6,7},{7,8},{8,9},{9,10},{10,1... | collective-permute-start | bytes 6291464 | tf_op jit(solution)/shard_map/while/body/eval_jaxpr/ppermute | solution.py:27
  749.1 23.7 collective-permute-start
  779.4 23.7 collective-permute-start
  809.7 25.4 collective-permute-start
  841.7 33.9 collective-permute-start
  882.4 25.5 collective-permute-start
  966.1 67.3 %while.47 = (s32[]{:T(128)}, f32[8,256,256]{2,1,0:T(8,128)}, f32[8,256]{1,0:T(8,128)S(1)}, s32[8]{0:T(128)S(1)}, bf16[256,2048]{0,1:T(8,128)(2,1)S(1)}, /*index=...) while((s32[]{:T(128)}, f32[8,256,256]{2,1,0:T(8,128)}, ...), condition=%wide.region_12.13_spmd.clone, body=%wide.region_9.12_spmd.clone.sunk | while | flops 1153105664 | bytes 27189480 | solution.py:197
  1090.2 605.2 %while.46 = (s32[]{:T(128)}, f32[256,2048]{0,1:T(8,128)}, f32[2,256,2048]{1,2,0:T(8,128)}, s32[16]{0:T(128)S(1)}, bf16[17,256,2048]{2,1,0:T(8,128)(2,1)}, /*inde...) while((s32[]{:T(128)}, f32[256,2048]{0,1:T(8,128)}, ...), condition=%wide.region_17.18_spmd, body=%wide.region_16.17_spmd.sunk | while | flops 1351614464 | bytes 105071040 | solution.py:282
  1782.3 33.3 convert_reduce_fusion
  1828.4 25.5 fusion.55
  1893.2 25.6 convolution_bitcast_fusion
  1918.8 130.9 %pad_maximum_fusion = f32[2048,24576]{1,0:T(8,128)} fusion(f32[2048,8192]{1,0:T(8,128)} %convolution_bitcast_fusion, f32[2048,2048]{1,0:T(8,128)} %convolution_bitcast_fusion.1, f32[2048,8192]{1,0:T(8,128)} %fusion.55, f32[2048,6144]{1,0:T(8,128)} %fusion.58), kind=kLoop, calls=%fused_computation.30 | loop fusion | flops 150994944 | bytes 402653184 | tf_op jit(solution)/shard_map/concatenate | solution.py:310
  2075.9 75.3 %reduce-scatter.7.cloned.1.call-done = f32[64,13]{1,0:T(8,128)} async-done(((f32[2048,13]{1,0:T(8,128)}), f32[64,13]{1,0:T(8,128)}) %reduce-scatter.7.cloned.1.call-update) | async-done | bytes 3344
  2152.6 1620.6 %reduce-scatter.5.cloned.1.call-done = f32[64,24576]{1,0:T(8,128)} async-done(((f32[2048,24576]{1,0:T(8,128)}), f32[64,24576]{1,0:T(8,128)}) %reduce-scatter.5.cloned.1.call-update) | async-done | bytes 6291472 | tf_op jit(solution)/shard_map/reduce_scatter | solution.py:309
  (812 shorter events, 1151.7 us)
Async XLA Ops:
  7.2 85.1 %all-gather.8.cloned.1.call-start = ((), (), s32[]{:S(2)}) async-start(), calls=%async_computation.3 | async-start | bytes 8650752 | tf_op jit(solution)/shard_map/all_gather | solution.py:202
  9.2 239.9 %all-gather.6.cloned.1.call-start = ((), (), s32[]{:S(2)}) async-start(), calls=%async_computation.2 | async-start | bytes 25952256 | tf_op jit(solution)/shard_map/all_gather | solution.py:146
  11.6 1753.5 %all-gather.10.cloned.1.call-start = ((), (), s32[]{:S(2)}) async-start(), calls=%async_computation.4 | async-start | bytes 34603008 | tf_op jit(solution)/shard_map/all_gather | solution.py:147
  12.8 1769.5 %all-gather.12.cloned.1.call-start = ((), (), s32[]{:S(2)}) async-start(), calls=%async_computation.5 | async-start | bytes 34603008 | tf_op jit(solution)/shard_map/all_gather | solution.py:203
  15.6 2135.5 %reduce-scatter.7.cloned.1.call-start = ((), (), s32[]{:S(2)}) async-start(), calls=%async_computation.7 | async-start | bytes 1081344
  286.0 49.1 %collective-permute-start = (bf16[2,256,2048]{2,1,0:T(8,128)(2,1)}, bf16[2,256,2048]{2,1,0:T(8,128)(2,1)S(1)}, u32[]{:S(2)}, u32[]{:S(2)}) collective-permute-start(bf16[2,256,2048]{2,1,0:T(8,128)(2,1)} %get-tuple-element.627), channel_id=1, source_target_pairs={{0,1},{1,2},{2,3},{3,4},{4,5},{5,6},{6,7},{7,8},{8,9},{9,10},{10,1... | collective-permute-start | bytes 6291464 | tf_op jit(solution)/shard_map/while/body/eval_jaxpr/ppermute | solution.py:27
  337.9 30.5 collective-permute-start
  371.2 69.5 %collective-permute-start = (bf16[2,256,2048]{2,1,0:T(8,128)(2,1)}, bf16[2,256,2048]{2,1,0:T(8,128)(2,1)S(1)}, u32[]{:S(2)}, u32[]{:S(2)}) collective-permute-start(bf16[2,256,2048]{2,1,0:T(8,128)(2,1)} %get-tuple-element.627), channel_id=1, source_target_pairs={{0,1},{1,2},{2,3},{3,4},{4,5},{5,6},{6,7},{7,8},{8,9},{9,10},{10,1... | collective-permute-start | bytes 6291464 | tf_op jit(solution)/shard_map/while/body/eval_jaxpr/ppermute | solution.py:27
  443.5 31.3 collective-permute-start
  507.9 35.1 collective-permute-start
  545.8 57.5 %collective-permute-start = (bf16[2,256,2048]{2,1,0:T(8,128)(2,1)}, bf16[2,256,2048]{2,1,0:T(8,128)(2,1)S(1)}, u32[]{:S(2)}, u32[]{:S(2)}) collective-permute-start(bf16[2,256,2048]{2,1,0:T(8,128)(2,1)} %get-tuple-element.627), channel_id=1, source_target_pairs={{0,1},{1,2},{2,3},{3,4},{4,5},{5,6},{6,7},{7,8},{8,9},{9,10},{10,1... | collective-permute-start | bytes 6291464 | tf_op jit(solution)/shard_map/while/body/eval_jaxpr/ppermute | solution.py:27
  606.1 53.0 %collective-permute-start = (bf16[2,256,2048]{2,1,0:T(8,128)(2,1)}, bf16[2,256,2048]{2,1,0:T(8,128)(2,1)S(1)}, u32[]{:S(2)}, u32[]{:S(2)}) collective-permute-start(bf16[2,256,2048]{2,1,0:T(8,128)(2,1)} %get-tuple-element.627), channel_id=1, source_target_pairs={{0,1},{1,2},{2,3},{3,4},{4,5},{5,6},{6,7},{7,8},{8,9},{9,10},{10,1... | collective-permute-start | bytes 6291464 | tf_op jit(solution)/shard_map/while/body/eval_jaxpr/ppermute | solution.py:27
  661.9 55.7 %collective-permute-start = (bf16[2,256,2048]{2,1,0:T(8,128)(2,1)}, bf16[2,256,2048]{2,1,0:T(8,128)(2,1)S(1)}, u32[]{:S(2)}, u32[]{:S(2)}) collective-permute-start(bf16[2,256,2048]{2,1,0:T(8,128)(2,1)} %get-tuple-element.627), channel_id=1, source_target_pairs={{0,1},{1,2},{2,3},{3,4},{4,5},{5,6},{6,7},{7,8},{8,9},{9,10},{10,1... | collective-permute-start | bytes 6291464 | tf_op jit(solution)/shard_map/while/body/eval_jaxpr/ppermute | solution.py:27
  841.7 37.8 collective-permute-start
  1132.1 30.0 collective-permute-start.1
  1170.3 29.5 collective-permute-start.1
  1208.0 30.1 collective-permute-start.1
  1283.8 30.2 collective-permute-start.1
  1359.8 30.1 collective-permute-start.1
  1398.1 29.5 collective-permute-start.1
  1435.8 29.5 collective-permute-start.1
  1473.5 29.5 collective-permute-start.1
  1511.1 29.5 collective-permute-start.1
  1893.2 1880.0 %reduce-scatter.5.cloned.1.call-start = ((), (), s32[]{:S(2)}) async-start(), calls=%async_computation.6 | async-start | bytes 207618048 | tf_op jit(solution)/shard_map/reduce_scatter | solution.py:309
  (174 other events, 9547.3 us)
Sparse Core Ops, SparseCore 0:
  11.5 80.7 all-gather.7
  95.7 153.2 all-gather.5
  252.5 232.3 all-gather.9
  488.2 247.7 all-gather.11
  1893.3 257.7 reduce-scatter.6
  2158.5 1614.5 reduce-scatter.4
where the time goes:
time: 3810 us; the launch traced here: 3800 us
  waiting for transfers between devices  2030 us (53%)
  starting transfers between devices  547 us (14%)
  matrix products  390 us (10%)
  other arithmetic  367 us (10%)
  local copies, waits for them, and re-layouts  357 us (9%)
  loops' own time  48.5 us (1%)
  blocking collectives  44.6 us (1%)
    reduce_scatter x1, waiting for transfers between devices, body(): lax.psum_scatter(jnp.concatenate([contract_rows(cols_one, grad_joint), co...  1620 us
    ppermute x32, starting transfers between devices, shifted(): return lax.ppermute(value, axis, pairs)  547 us
    ppermute x32, waiting for transfers between devices, shifted(): return lax.ppermute(value, axis, pairs)  163 us
    all_gather x1, waiting for transfers between devices, body(): lax.all_gather(inner_low, 'fsdp', axis=0, tiled=True)  148 us
    concatenate x1, other arithmetic, body(): jnp.concatenate([contract_rows(cols_one, grad_joint), contract_rows(cols_...  131 us
    dot_general x4, matrix products, contract_rows(): lax.dot_general(left, right, (((0,), (0,)), ((), ())), preferred_element_...  80.3 us
  transfers between devices with their start and end apart: 38, of which 36 were waited for; matrix products, arithmetic and copies ran while one was open for 25% of the time, Pallas kernels for 0%

commit v1 on v0

v1 whole, which is shorter than its diff:
```python
import math

import jax
import jax.numpy as jnp
from jax import lax
from jax.experimental import pallas as pl
from jax.experimental.pallas import tpu as pltpu
from jax.sharding import PartitionSpec as P

D = 2048
HEADS = 8
HEAD = D // HEADS
FF = 8192
FFT = FF // HEADS
LMAX = 4096
STEPS = 10
TOK = 256
RUN = 2 * TOK
BACK_RUNS = LMAX // RUN + 1

NORM_EPS = 1e-05
ADAM_EPS = 1e-08
BETA_ONE = 0.9
BETA_TWO = 0.95
WEIGHT_DECAY = 0.01
NEGATIVE = -1e30
ROPE_BASE = 10000.0
SMALLC = 13
SMALLR = 16

BF = jnp.bfloat16
F32 = jnp.float32
ANY = pl.BlockSpec(memory_space=pl.ANY)
VM = pl.BlockSpec(memory_space=pltpu.VMEM)
MIB = 1024 * 1024
WEIGHTS = ((3, HEAD), (1, FFT), (1, HEAD), (1, FFT))


class Place:
    def __init__(self, n):
        self.n = n
        self.S = n // 4
        self.R = self.S // 2
        self.bits = int(math.log2(self.R))
        me = lax.axis_index("fsdp")
        self.me = me
        self.zt = me // self.S
        self.rr = (me % self.S) // 2
        self.c = me % 2
        self.z1 = self.zt // 2
        self.z0 = self.zt % 2
        self.t = self.zt * 2 + self.c

    def zt_of(self, s):
        z1 = 1 - self.z1 if s & 1 else self.z1
        z0 = 1 - self.z0 if s & 2 else self.z0
        return z1 * 2 + z0

    def zt_of_run(self, u):
        z1 = self.z1 + (1 - 2 * self.z1) * (u % 2)
        z0 = self.z0 + (1 - 2 * self.z0) * (u // 2)
        return z1 * 2 + z0

    def c_of(self, s):
        return 1 - self.c if s & 4 else self.c

    def t_of(self, s):
        return self.zt_of(s) * 2 + self.c_of(s)

    def rr_of(self, i):
        out = 0
        for k in range(self.bits):
            bit = (self.rr // (1 << k)) % 2
            out = out + (1 - bit if i >> k & 1 else bit) * (1 << k)
        return out

    def dev_t(self, s):
        return self.zt_of(s) * self.S + self.rr * 2 + self.c_of(s)

    def dev_r(self, i):
        return self.zt * self.S + self.rr_of(i) * 2 + self.c


class Copies:
    def __init__(self, send, recv):
        self.send, self.recv, self.count, self.started = send, recv, 0, []

    def remote(self, src, dst, dev):
        k = self.count
        self.count += 1
        copy = pltpu.make_async_remote_copy(
            src_ref=src,
            dst_ref=dst,
            send_sem=self.send.at[k],
            recv_sem=self.recv.at[k],
            device_id=(dev,),
            device_id_type=pl.DeviceIdType.MESH,
        )
        copy.start()
        self.started.append(copy)
        return copy

    def local(self, src, dst):
        k = self.count
        self.count += 1
        copy = pltpu.make_async_copy(src, dst, self.send.at[k])
        copy.start()
        return copy

    def finish(self):
        for copy in self.started:
            copy.wait_send()


def greet(place, t_group, r_group):
    barrier = pltpu.get_barrier_semaphore()
    peers = [place.dev_t(s) for s in t_group] + [place.dev_r(i) for i in r_group]
    for dev in peers:
        pl.semaphore_signal(barrier, inc=1, device_id=(dev,), device_id_type=pl.DeviceIdType.MESH)
    pl.semaphore_wait(barrier, len(peers))


def top_bit(s):
    return 1 << (s.bit_length() - 1)


def orders(bits):
    up = [1 << k for k in range(bits)]
    return [up, up[::-1]]


def spread(order):
    have, out = [0], []
    for bit in order:
        new = [i | bit for i in have]
        out += [(i, bit) for i in new]
        have = have + new
    return out


def collected(order):
    left, out = list(range(1 << len(order))), []
    for bit in order:
        out.append((bit, [i for i in left if i & bit]))
        left = [i for i in left if not i & bit]
    return out


def add_rows(dst, a, b):
    lead = dst.shape[:-2]
    rows, columns = dst.shape[-2:]
    size = min(rows, max(16, 1 << int(math.log2(16384 // columns))))
    for flat in range(math.prod(lead)):
        where, rest = [], flat
        for extent in lead[::-1]:
            where.insert(0, rest % extent)
            rest //= extent

        def step(k, carry, where=tuple(where)):
            at = where + (pl.ds(pl.multiple_of(k * size, size), size), slice(None))
            dst[at] = (a[at].astype(F32) + b[at].astype(F32)).astype(dst.dtype)
            return carry

        lax.fori_loop(0, rows // size, step, 0)


def call(kernel, ins, in_specs, outs, out_specs, scratch, collective_id, copies, vmem=60):
    return pl.pallas_call(
        kernel,
        out_shape=outs,
        in_specs=in_specs,
        out_specs=out_specs,
        scratch_shapes=[
            *scratch,
            pltpu.SemaphoreType.DMA((copies,)),
            pltpu.SemaphoreType.DMA((copies,)),
        ],
        compiler_params=pltpu.CompilerParams(
            collective_id=collective_id, has_side_effects=True, vmem_limit_bytes=vmem * MIB
        ),
    )(*ins)


class Net:
    def __init__(self, send, recv):
        self.send, self.recv, self.makers, self.count = send, recv, [], 0

    def add(self, maker, many=1):
        base = self.count
        self.count += many

        def build(k=0):
            src, dst, dev = maker(k)
            return pltpu.make_async_remote_copy(
                src_ref=src,
                dst_ref=dst,
                send_sem=self.send.at[base + k],
                recv_sem=self.recv.at[base + k],
                device_id=(dev,),
                device_id_type=pl.DeviceIdType.MESH,
            )

        self.makers.append((build, many))
        return build

    def finish(self):
        for build, many in self.makers:
            if many == 1:
                build().wait_send()
            else:

                def one(k, carry, build=build):
                    build(k).wait_send()
                    return carry

                lax.fori_loop(0, many, one, 0)


class GatherT:
    def __init__(self, net, place, own, out):
        self.ops = {}
        for s in range(1, 8):
            hop = top_bit(s)
            src = own if s == hop else out.at[(s - hop) // 4, (s - hop) % 4]
            self.ops[s] = net.add(
                lambda k, src=src, s=s, hop=hop: (src, out.at[s // 4, s % 4], place.dev_t(hop))
            )

    def start(self, *which):
        for s in which:
            self.ops[s]().start()

    def wait(self, *which):
        for s in which:
            self.ops[s]().wait_recv()


class GatherR:
    def __init__(self, net, place, region, order):
        self.plan = spread(order)
        self.ops = {}
        self.later = [(i, bit) for i, bit in self.plan if i != bit]
        self.used = {i ^ bit for i, bit in self.later}
        for i, bit in self.plan:
            self.ops[i] = net.add(
                lambda k, i=i, bit=bit: (region(i ^ bit), region(i ^ bit), place.dev_r(bit))
            )

    def begin(self):
        for i, bit in self.plan:
            if i == bit:
                self.ops[i]().start()

    def advance(self):
        seen = set()
        for i, bit in self.later:
            if i ^ bit not in seen:
                self.ops[i ^ bit]().wait_recv()
                seen.add(i ^ bit)
            self.ops[i]().start()

    def end(self):
        for i, _ in self.plan:
            if i not in self.used:
                self.ops[i]().wait_recv()


def cosine_and_sine(x):
    turns = jnp.floor(x * (2.0 / math.pi) + 0.5)
    r = ((x - turns * 1.5703125) - turns * 4.837512969970703e-4) - turns * 7.549789954891882e-8
    z = r * r
    sine = ((-1.9515295891e-4 * z + 8.3321608736e-3) * z - 1.6666654611e-1) * z * r + r
    cosine = (
        ((2.443315711809948e-5 * z - 1.388731625493765e-3) * z + 4.166664568298827e-2) * z * z
        - 0.5 * z
        + 1.0
    )
    quarter = turns - 4.0 * jnp.floor(turns * 0.25)
    odd = (quarter == 1.0) | (quarter == 3.0)
    first, second = jnp.where(odd, sine, cosine), jnp.where(odd, cosine, sine)
    return (
        jnp.where((quarter == 1.0) | (quarter == 2.0), -first, first),
        jnp.where(quarter >= 2.0, -second, second),
    )


def shuffle_matrix():
    turned, half = HEAD // 8, HEAD // 2
    into = lax.broadcasted_iota(jnp.int32, (HEAD, HEAD), 1)
    source = lax.broadcasted_iota(jnp.int32, (HEAD, HEAD), 0)
    moved = jnp.where((into >= turned) & (into < half), into + turned, into)
    moved = jnp.where((into >= half) & (into < half + turned), into - (half - turned), moved)
    return jnp.where(source == moved, 1.0, 0.0).astype(F32)


def weight_halves(net, place, ref):
    both = orders(place.bits)
    return [
        GatherR(net, place, lambda i, h=h: ref.at[pl.ds(2 * h, 2), place.rr_of(i)], both[h])
        for h in range(2)
    ]


def forward_kernel(
    n, nseq, x, gy, wi, wu, wo, wd, small, lengths, frequency,
    xg, gg, a1g, a2g, oi, ou, oo, od, qo, kg, vg, zo, dho, dout, smt, sums, stats, cosine, sine,
    xv, gv, sm, ti, tu, to, td, slope, a2v, kt, vt, at, ztile, dht, bias, dhsum,
    send, recv, local, out_sem, g_sem,
):
    place = Place(n)
    rb = D // n
    net = Net(send, recv)
    weights = list(zip((wi, wu, wo, wd), (ti, tu, to, td), WEIGHTS))
    greet(place, range(1, 8), [1 << k for k in range(place.bits)])
    mine = pl.ds(pl.multiple_of(place.c * rb, rb), rb)

    small_t = [
        net.add(lambda k, s=s: (small, sm.at[place.zt, place.rr, mine, :], place.dev_t(s)))
        for s in range(1, 8)
    ]

    def columns(p, width, t):
        return pl.ds(pl.multiple_of(p * D + t * width, 128), width)

    def exchange(which):
        src, dst, (parts, width) = weights[which]
        return [
            net.add(
                lambda k, s=s, p=p: (
                    src.at[:, columns(p, width, place.t_of(s))],
                    dst.at[place.zt, place.rr, mine, pl.ds(p * width, width)],
                    place.dev_t(s),
                )
            )
            for s in range(1, 8)
            for p in range(parts)
        ]

    to_t = [exchange(k) for k in range(4)]
    small_r = GatherR(net, place, lambda i: sm.at[:, place.rr_of(i)], orders(place.bits)[0])
    to_r = [weight_halves(net, place, w[1]) for w in weights]
    x_t = GatherT(net, place, x, xv)
    g_t = GatherT(net, place, gy, gv)
    both = orders(place.bits)
    keys = []
    for own, out, order in ((kt, kg, both[0]), (vt, vg, both[1])):
        ops = {}
        for i, bit in spread(order):
            ops[i] = net.add(
                lambda s, i=i, bit=bit, own=own, out=out: (
                    own.at[s // 4, s % 4] if i == bit else out.at[i ^ bit, s // 4, s % 4],
                    out.at[i, s // 4, s % 4],
                    place.dev_r(bit),
                ),
                8,
            )
        keys.append((ops, spread(order)))

    def start(ops):
        for op in ops:
            op().start()

    def wait(ops):
        for op in ops:
            op().wait_recv()

    locals_ = [
        pltpu.make_async_copy(x, xv.at[0, 0], local.at[0]),
        pltpu.make_async_copy(gy, gv.at[0, 0], local.at[1]),
        pltpu.make_async_copy(small, sm.at[place.zt, place.rr, mine, :], local.at[2]),
    ]
    for src, dst, (parts, width) in weights:
        for p in range(parts):
            locals_.append(
                pltpu.make_async_copy(
                    src.at[:, columns(p, width, place.t)],
                    dst.at[place.zt, place.rr, mine, pl.ds(p * width, width)],
                    local.at[len(locals_)],
                )
            )
    for copy in locals_:
        copy.start()
    start(small_t)
    start(to_t[0])
    x_t.start(4)
    for copy in locals_:
        copy.wait()
    wait(small_t)
    small_r.begin()
    wait(to_t[0])
    for part in to_r[0]:
        part.begin()
    start(to_t[1])
    x_t.start(2, 1)
    small_r.advance()
    for part in to_r[0]:
        part.advance()

    def tables(s, carry):
        core, u = s // 4, s % 4
        device = (
            place.zt_of_run(u) * place.S + place.rr * 2 + place.c + (1 - 2 * place.c) * core
        )
        token = device * TOK + lax.broadcasted_iota(jnp.int32, (TOK, HEAD // 2), 0)
        offset = token - start_of(token, lengths, nseq)
        angles = offset.astype(F32) * frequency[0:1, :]
        cosine[core, u], sine[core, u] = cosine_and_sine(angles)
        return carry

    lax.fori_loop(0, 8, tables, 0)
    wait(to_t[1])
    for part in to_r[1]:
        part.begin()
    start(to_t[3])
    start(to_t[2])
    small_r.end()

    smt[...] = sm[...].reshape(D, 128).T[:SMALLR, :]
    head_cols = pl.ds(pl.multiple_of(place.t * HEAD, HEAD), HEAD)
    shuffle = shuffle_matrix()
    three = jnp.dot(
        smt[0:8, head_cols], shuffle, precision=lax.Precision.HIGHEST, preferred_element_type=F32
    )
    for p in range(2):
        bias[0:1, p * HEAD : (p + 1) * HEAD] = three[4 + p : 5 + p, :]
    bias[0:1, 2 * HEAD : 3 * HEAD] = smt[6:7, head_cols]

    def repeat_matrix():
        lane = lax.broadcasted_iota(jnp.int32, (HEAD, FFT), 1)
        row = lax.broadcasted_iota(jnp.int32, (HEAD, FFT), 0)
        return jnp.where(lane // 4 == row, 1.0, 0.0).astype(F32)

    four = jnp.dot(
        smt[8:16, head_cols],
        repeat_matrix(),
        precision=lax.Precision.HIGHEST,
        preferred_element_type=F32,
    )
    lane8 = lax.broadcasted_iota(jnp.int32, (8, FFT), 1)
    row8 = lax.broadcasted_iota(jnp.int32, (8, FFT), 0)
    bias[1:2, :] = jnp.sum(jnp.where(lane8 % 4 + 1 == row8, four, 0.0), axis=0, keepdims=True)

    for part in to_r[0]:
        part.end()
    copy_out = [pltpu.make_async_copy(ti, oi, local.at[0])]
    copy_out[0].start()

    def norms(u):
        def chunk(r, carry):
            at_rows = (r // 16, pl.ds(pl.multiple_of(r % 16 * 16, 16), 16), slice(None))
            in_rows = (at_rows[0], u, *at_rows[1:])
            xf = xv[in_rows].astype(F32)
            average = jnp.mean(xf, axis=1, keepdims=True)
            centred = xf - average
            var = jnp.mean(centred * centred, axis=1, keepdims=True)
            inverse = lax.rsqrt(var + NORM_EPS)
            xhat = centred * inverse
            at[at_rows] = (xhat * smt[0:1, :] + smt[1:2, :]).astype(BF)
            a2v[in_rows] = (xhat * smt[2:3, :] + smt[3:4, :]).astype(BF)
            lanes = lax.broadcasted_iota(jnp.int32, (16, 128), 1)
            stats[in_rows] = jnp.where(lanes == 0, average, inverse)
            return carry

        lax.fori_loop(0, 2 * TOK // 16, chunk, 0, unroll=4)

    def place_of(k):
        return k % 2 * 2 + k // 2

    def events(k, table):
        for when, what in table.items():

            @pl.when(k == when)
            def _(what=what):
                for fn in what:
                    fn()

    def staged(buffer, out, u, sem):
        return pltpu.make_async_copy(buffer, out.at[:, u], out_sem.at[sem])

    def free(buffer, out, k, sem):
        @pl.when(k >= 1)
        def _():
            staged(buffer, out, 0, sem).wait()

    def forward_keys(s):
        for ops, plan in keys:
            seen = set()
            for i, bit in plan:
                if i != bit:
                    if i ^ bit not in seen:
                        ops[i ^ bit](s).wait_recv()
                        seen.add(i ^ bit)
                    ops[i](s).start()

    def hidden_units(k):
        u = place_of(k)
        hidden = jnp.dot(
            a2v[:, u].reshape(RUN, D), tu[...].reshape(D, FFT), preferred_element_type=F32
        )
        slope[:, u] = (hidden + bias[1:2, :]).reshape(2, TOK, FFT)
        free(ztile, zo, k, 1)

        def chunk(r, carry):
            at_rows = (r // 16, pl.ds(pl.multiple_of(r % 16 * 16, 16), 16), slice(None))
            in_rows = (at_rows[0], u, *at_rows[1:])
            h = slope[in_rows]
            bell = jnp.exp(-0.5 * h * h)
            t = 1.0 / (1.0 + (0.3275911 * 0.5**0.5) * jnp.abs(h))
            series = t * (
                0.254829592
                + t * (-0.284496736 + t * (1.421413741 + t * (-1.453152027 + t * 1.061405429)))
            )
            tail = 0.5 * series * bell
            phi = jnp.where(h < 0.0, tail, 1.0 - tail)
            ztile[at_rows] = (h * phi).astype(BF)
            slope[in_rows] = phi + h * bell * (1.0 / math.sqrt(2.0 * math.pi))
            return carry

        lax.fori_loop(0, 2 * TOK // 16, chunk, 0, unroll=2)
        staged(ztile, zo, u, 1).start()

    def projections(k):
        u = place_of(k)
        free(at, a1g, k, 0)
        norms(u)
        joint = (
            jnp.dot(
                at[...].reshape(RUN, D), ti[...].reshape(D, 3 * HEAD), preferred_element_type=F32
            )
            + bias[0:1, : 3 * HEAD]
        )
        staged(at, a1g, u, 0).start()
        half = HEAD // 2
        cs, sn = cosine[:, u].reshape(RUN, half), sine[:, u].reshape(RUN, half)
        for p, (dst, scale) in enumerate(((qo, HEAD**-0.5), (kt, None))):
            one = joint[:, p * HEAD : p * HEAD + half]
            two = joint[:, p * HEAD + half : (p + 1) * HEAD]
            for at_col, value in ((0, one * cs - two * sn), (half, two * cs + one * sn)):
                value = value.astype(BF)
                if scale is not None:
                    value = (value.astype(F32) * scale).astype(BF)
                dst[:, u, :, at_col : at_col + half] = value.reshape(2, TOK, half)
        vt[:, u] = joint[:, 2 * HEAD :].astype(BF).reshape(2, TOK, HEAD)
        for core in range(2):
            for ops, plan in keys:
                for i, bit in plan:
                    if i == bit:
                        ops[i](core * 4 + u).start()

    def first(k, carry):
        events(
            k,
            {
                0: [lambda: x_t.wait(4)],
                1: [
                    lambda: [p.advance() for p in to_r[1]],
                    lambda: x_t.wait(2),
                    lambda: x_t.start(6),
                    lambda: x_t.wait(6),
                ],
                2: [
                    lambda: x_t.wait(1),
                    lambda: x_t.start(3, 5),
                    lambda: [p.end() for p in to_r[1]],
                    lambda: pltpu.make_async_copy(tu, ou, local.at[1]).start(),
                ],
                3: [
                    lambda: wait(to_t[3]),
                    lambda: wait(to_t[2]),
                    lambda: [p.begin() for p in to_r[3] + to_r[2]],
                    lambda: g_t.start(1, 4),
                ],
                4: [lambda: x_t.wait(5)],
                5: [
                    lambda: [p.advance() for p in to_r[3] + to_r[2]],
                    lambda: x_t.wait(3),
                    lambda: x_t.start(7),
                    lambda: g_t.start(2),
                    lambda: x_t.wait(7),
                ],
                7: [lambda: g_t.wait(1), lambda: g_t.start(3, 5)],
            },
        )
        late = k // 4

        @pl.when(k % 4 < 2)
        def _():
            projections(k - 2 * late)

        @pl.when(k % 4 >= 2)
        def _():
            hidden_units(k - 2 - 2 * late)

        @pl.when((k == 3) | (k >= 5))
        def _():
            pair = k - 3 - late
            for core in range(2):
                forward_keys(core * 4 + place_of(pair))

        return carry

    lax.fori_loop(0, 8, first, 0)
    own_out = [
        pltpu.make_async_copy(kt, kg.at[0], local.at[4]),
        pltpu.make_async_copy(vt, vg.at[0], local.at[5]),
        pltpu.make_async_copy(xv, xg, local.at[6]),
        pltpu.make_async_copy(a2v, a2g, local.at[8]),
    ]
    for copy in own_out:
        copy.start()
    copy_out.append(pltpu.make_async_copy(tu, ou, local.at[1]))

    def finish_keys(s, carry):
        for ops, plan in keys:
            used = {i ^ bit for i, bit in plan if i != bit}
            for i, bit in plan:
                if i not in used:
                    ops[i](s).wait_recv()
        return carry

    for part in to_r[3] + to_r[2]:
        part.end()
    copy_out += [
        pltpu.make_async_copy(to, oo, local.at[2]),
        pltpu.make_async_copy(td, od, local.at[3]),
    ]
    copy_out[2].start()
    copy_out[3].start()
    dhsum[...] = jnp.zeros_like(dhsum)

    def third(k, carry):
        u = place_of(k)
        events(
            k,
            {
                0: [lambda: g_t.wait(4)],
                1: [lambda: g_t.wait(2), lambda: g_t.start(6), lambda: g_t.wait(6)],
                2: [lambda: g_t.wait(5)],
                3: [lambda: g_t.wait(3), lambda: g_t.start(7), lambda: g_t.wait(7)],
            },
        )
        free(dht, dho, k, 2)
        pltpu.make_async_copy(gv.at[:, u], gg.at[:, u], g_sem.at[u]).start()
        grad = gv[:, u].reshape(RUN, D)
        dz = jnp.dot(grad, td[...].reshape(D, FFT), preferred_element_type=F32)
        dh = (dz * slope[:, u].reshape(RUN, FFT)).astype(BF)
        dht[...] = dh.reshape(2, TOK, FFT)
        staged(dht, dho, u, 2).start()
        dhsum[0:1, :] += jnp.sum(dh.astype(F32), axis=0, keepdims=True)
        dout[:, u] = (
            jnp.dot(grad, to[...].reshape(D, HEAD), preferred_element_type=F32)
            .astype(BF)
            .reshape(2, TOK, HEAD)
        )
        return carry

    lax.fori_loop(0, 4, third, 0)
    four = jnp.dot(
        jnp.where(lane8 % 4 + 1 == row8, dhsum[0:1, :], 0.0),
        repeat_matrix().T,
        precision=lax.Precision.HIGHEST,
        preferred_element_type=F32,
    )
    sums[...] = jnp.zeros_like(sums)
    sums[8:16, head_cols] = four
    sums[8:9, :] = jnp.sum(gv[0, 0].astype(F32), axis=0, keepdims=True)
    sums[7:8, :] = sums[8:9, :]
    lax.fori_loop(0, 8, finish_keys, 0)
    for sem, (buffer, out) in enumerate(((at, a1g), (ztile, zo), (dht, dho))):
        staged(buffer, out, 0, sem).wait()
    for copy in copy_out + own_out:
        copy.wait()
    for u in range(4):
        pltpu.make_async_copy(gv.at[:, u], gg.at[:, u], g_sem.at[u]).wait()
    net.finish()


def forward(n, x, gy, weights, small, lengths, frequency):
    rb = D // n
    R = n // 8

    def shape(*dims, kind=BF):
        return jax.ShapeDtypeStruct(dims, kind)

    w_shapes = [(4, R, 2 * rb, parts * width) for parts, width in WEIGHTS]
    block, cols, head = (2, 4, TOK, D), (2, 4, TOK, FFT), (2, 4, TOK, HEAD)
    outs = [shape(*block) for _ in range(4)]
    outs += [shape(*w) for w in w_shapes]
    outs += [shape(*head), shape(R, *head), shape(R, *head), shape(*cols), shape(*cols)]
    outs += [shape(*head), shape(SMALLR, D, kind=F32), shape(SMALLR, D, kind=F32)]
    outs += [shape(2, 4, TOK, 128, kind=F32)]
    outs += [shape(2, 4, TOK, HEAD // 2, kind=F32) for _ in range(2)]
    out_specs = [ANY] * 8 + [VM] + [ANY] * 4 + [VM] * 6
    scratch = [
        pltpu.VMEM(block, BF),
        pltpu.VMEM(block, BF),
        pltpu.VMEM((4, R, 2 * rb, 128), F32),
        *[pltpu.VMEM(w, BF) for w in w_shapes],
        pltpu.VMEM(cols, F32),
        pltpu.VMEM(block, BF),
        pltpu.VMEM(head, BF),
        pltpu.VMEM(head, BF),
        pltpu.VMEM((2, TOK, D), BF),
        pltpu.VMEM((2, TOK, FFT), BF),
        pltpu.VMEM((2, TOK, FFT), BF),
        pltpu.VMEM((8, FFT), F32),
        pltpu.VMEM((8, FFT), F32),
    ]
    copies = 7 + 7 * 6 + (R - 1) * (1 + 8 + 2 * 8) + 14

    def kernel(*refs):
        forward_kernel(n, lengths.shape[0], *refs)

    return pl.pallas_call(
        kernel,
        out_shape=outs,
        in_specs=[ANY] * 7 + [pl.BlockSpec(memory_space=pltpu.SMEM), VM],
        out_specs=out_specs,
        scratch_shapes=[
            *scratch,
            pltpu.SemaphoreType.DMA((copies,)),
            pltpu.SemaphoreType.DMA((copies,)),
            pltpu.SemaphoreType.DMA((16,)),
            pltpu.SemaphoreType.DMA((3,)),
            pltpu.SemaphoreType.DMA((4,)),
        ],
        compiler_params=pltpu.CompilerParams(
            collective_id=0, has_side_effects=True, vmem_limit_bytes=62 * MIB
        ),
    )(x, gy, *weights, small, lengths, frequency)


class SumT:
    def __init__(self, copies, place, data, slots, out):
        self.copies, self.place, self.data, self.slots, self.out = copies, place, data, slots, out
        self.ops = {}
        self.cur = {s: data.at[s] for s in range(8)}

    def send(self, s):
        hop = top_bit(s)
        self.ops[s] = self.copies.remote(self.cur[s], self.slots.at[s - 1], self.place.dev_t(hop))

    def add(self, s):
        to = s - top_bit(s)
        self.ops[s].wait_recv()
        slot = self.slots.at[s - 1]
        if to == 0 and s == 1:
            add_rows(self.out, self.cur[0], slot)
        else:
            add_rows(slot, self.cur[to], slot)
            self.cur[to] = slot

    def start(self):
        for s in (6, 7, 5, 4):
            self.send(s)

    def middle(self):
        for s in (6, 7):
            self.add(s)
            self.send(s - 4)
        self.add(5)

    def late(self):
        self.add(3)
        self.send(1)
        self.add(4)
        self.add(2)

    def end(self):
        self.add(1)


class SumR:
    def __init__(self, copies, place, piece, slots, order):
        self.copies, self.place, self.slots = copies, place, slots
        self.steps = collected(order)
        self.cur = {i: piece(i) for i in range(1 << len(order))}
        self.ops = {}

    def send(self, step):
        bit, members = self.steps[step]
        for i in members:
            self.ops[i] = self.copies.remote(
                self.cur[i], self.slots.at[i - 1], self.place.dev_r(bit)
            )

    def add(self, step):
        bit, members = self.steps[step]
        for i in members:
            self.ops[i].wait_recv()
            slot = self.slots.at[i - 1]
            add_rows(slot, self.cur[i ^ bit], slot)
            self.cur[i ^ bit] = slot


def return_keys_kernel(n, have, *refs):
    place = Place(n)
    refs = list(refs)
    count = len(have)
    ins, refs = refs[:count], refs[count:]
    outs, refs = refs[:count], refs[count:]
    slots, (send, recv) = refs[:count], refs[count:]
    copies = Copies(send, recv)
    both = orders(place.bits)
    r_group = [1 << b for b in range(place.bits)] if set(have) - {"p"} else []
    t_group = (1, 2, 4) if "p" in have else ()
    greet(place, t_group, r_group)
    total, sums = None, []
    for name, src, dst, slot in zip(have, ins, outs, slots):
        if name == "p":
            total = SumT(copies, place, src, slot, dst)
        else:
            order = both[0] if name == "k" else both[1]
            sums.append((SumR(copies, place, lambda i, src=src: src.at[i], slot, order), dst))
    for part, _ in sums:
        part.send(0)
    if total:
        total.start()
        total.middle()
    for step in range(place.bits):
        for part, _ in sums:
            part.add(step)
            if step + 1 < place.bits:
                part.send(step + 1)
    if total:
        total.late()
    for part, dst in sums:
        copy = copies.local(part.cur[0], dst)
        copy.wait()
    if total:
        total.end()
    copies.finish()


def return_keys(n, ins, collective_id):
    R = n // 8
    outs, scratch, copies = [], [], 0
    for name in ins:
        if name == "p":
            outs.append(jax.ShapeDtypeStruct((TOK, D), F32))
            scratch.append(pltpu.VMEM((7, TOK, D), BF))
            copies += 7
        else:
            outs.append(jax.ShapeDtypeStruct((8, TOK, HEAD), BF))
            scratch.append(pltpu.VMEM((R - 1, 8, TOK, HEAD), BF))
            copies += R

    def kernel(*refs):
        return_keys_kernel(n, tuple(ins), *refs)

    out = call(
        kernel,
        tuple(ins.values()),
        [VM] * len(ins),
        outs,
        [VM] * len(ins),
        scratch,
        collective_id,
        copies,
    )
    return dict(zip(ins, out))


def return_grads_kernel(
    n, gi, gu, go, gd, e, small, oi, ou, oo, od, oe, osmall, si, su, so, sd, se, ss, send, recv
):
    place = Place(n)
    copies = Copies(send, recv)
    rb = D // n
    both = orders(place.bits)
    greet(place, range(1, 8), [1 << b for b in range(place.bits)])
    total = SumT(copies, place, e, se, oe)
    total.start()

    tasks = []
    for src, slot, dst, (parts, width) in zip(
        (gu, gd, gi, go), (su, sd, si, so), (ou, od, oi, oo), [WEIGHTS[k] for k in (1, 3, 0, 2)]
    ):
        for half in range(2):

            def piece(i, src=src, half=half):
                return src.at[pl.ds(2 * half, 2), place.rr_of(i)]

            part = SumR(copies, place, piece, slot.at[half], both[half])
            tasks.append((part, half, dst, parts, width))
    small_sum = SumR(copies, place, lambda i: small.at[:, place.rr_of(i)], ss, both[0])
    for part, *_ in tasks:
        part.send(0)
    small_sum.send(0)
    total.middle()
    for step in range(place.bits):
        for part, *_ in tasks:
            part.add(step)
            if step + 1 < place.bits:
                part.send(step + 1)
        small_sum.add(step)
        if step + 1 < place.bits:
            small_sum.send(step + 1)
    total.late()

    finals = {}
    for k in range(4):
        pieces = [tasks[2 * k + half][0].cur[0] for half in range(2)]
        finals[k] = pieces
    ops = []
    for k in range(4):
        _, _, dst, parts, width = tasks[2 * k]
        for zz in range(4):
            for cc in range(2):
                src = finals[k][zz // 2].at[zz % 2, pl.ds(cc * rb, rb), :]
                ops.append((zz, cc, src, dst, parts, width))
    sends = []
    for k in range(4):
        _, _, dst, parts, width = tasks[2 * k]
        store = tasks[2 * k][0].slots
        slot = store
        del slot
        for s in range(8):
            for p in range(parts):
                cols = pl.ds(pl.multiple_of(p * D + place.t * width, 128), width)
                sends.append((k, s, p, cols, dst, width))
    remote = []
    joined = {}
    for k, (ref, outbuf) in enumerate(((gu, ou), (gd, od), (gi, oi), (go, oo))):
        del ref, outbuf
        joined[k] = finals[k]
    for k, s, p, cols, dst, width in sends:
        base = (su, sd, si, so)[k]
        last = tasks[2 * k][0].steps[-1][1][0], tasks[2 * k + 1][0].steps[-1][1][0]
        zt = place.zt_of(s)
        rows = pl.ds(pl.multiple_of(place.c_of(s) * rb, rb), rb)
        which = zt // 2
        index = (1 - which) * (last[0] - 1) + which * (last[1] - 1)
        src = base.at[which, index, zt % 2, rows, pl.ds(p * width, width)]
        if s == 0:
            remote.append(("local", copies.local(src, dst.at[:, cols])))
        else:
            remote.append(("remote", copies.remote(src, dst.at[:, cols], place.dev_t(s))))
    last = small_sum.steps[-1][1][0] - 1
    for s in range(8):
        rows = pl.ds(pl.multiple_of(place.c_of(s) * SMALLR, SMALLR), SMALLR)
        src = ss.at[last, place.zt_of(s), rows, :]
        if s == 0:
            remote.append(("local", copies.local(src, osmall.at[place.t])))
        else:
            remote.append(("remote", copies.remote(src, osmall.at[place.t], place.dev_t(s))))
    total.end()
    for kind, copy in remote:
        if kind == "local":
            copy.wait()
        else:
            copy.wait_recv()
    copies.finish()


def return_grads(n, grads, e, small, collective_id):
    R = n // 8
    rb = D // n
    outs = [jax.ShapeDtypeStruct((rb, parts * D if parts > 1 else HEADS * width), BF) for parts, width in WEIGHTS]
    outs += [jax.ShapeDtypeStruct((TOK, D), F32), jax.ShapeDtypeStruct((8, SMALLR, 128), F32)]
    scratch = [
        pltpu.VMEM((2, R - 1, 2, 2 * rb, parts * width), BF) for parts, width in WEIGHTS
    ] + [
        pltpu.VMEM((7, TOK, D), BF),
        pltpu.VMEM((R - 1, 4, 2 * SMALLR, 128), F32),
    ]
    copies = 7 + 9 * (R - 1) + 8 * 6 + 8

    def kernel(*refs):
        return_grads_kernel(n, *refs)

    return call(
        kernel,
        (*grads, e, small),
        [VM] * 6,
        outs,
        [ANY] * 4 + [VM, ANY],
        scratch,
        collective_id,
        copies,
    )


WIDE = 512


class FoldT:
    def __init__(self, net, place, data, cs, zs, ys, out):
        self.data, self.cs, self.zs, self.ys, self.out = data, cs, zs, ys, out
        self.hop_c = net.add(lambda k: (data.at[k], cs.at[k], place.dev_t(4)), 4)
        self.hop_z0 = net.add(lambda k: (cs.at[2 + k], zs.at[k], place.dev_t(2)), 2)
        self.hop_z1 = net.add(lambda k: (zs.at[1], ys.at[0], place.dev_t(1)))

    @staticmethod
    def order(idx):
        return 7 - idx // 4 - 2 * (idx % 4)

    def loop(self, make, emit, after):
        def step(idx, carry):
            s = self.order(idx)
            make(s, idx)
            k = s % 4

            def far(where, value):
                self.data[(k, *where)] = value.astype(BF)

            def near(where, value):
                self.cs[(k, *where)] = (value + self.cs[(k, *where)].astype(F32)).astype(BF)

            @pl.when(s >= 4)
            def _():
                emit(s, idx, far)
                self.hop_c(k).start()

            @pl.when(s < 4)
            def _():
                self.hop_c(k).wait_recv()
                emit(s, idx, near)

                @pl.when(s >= 2)
                def _():
                    self.hop_z0(s - 2).start()

            after(idx)
            return carry

        lax.fori_loop(0, 8, step, 0)

    def turn_z1(self):
        self.hop_z0(1).wait_recv()
        add_rows(self.zs.at[1], self.cs.at[1], self.zs.at[1])
        self.hop_z1().start()

    def turn_own(self):
        self.hop_z0(0).wait_recv()
        add_rows(self.zs.at[0], self.cs.at[0], self.zs.at[0])

    def end(self):
        self.hop_z1().wait_recv()
        add_rows(self.out, self.zs.at[0], self.ys.at[0])


def fold_scratch():
    return [
        pltpu.VMEM((4, TOK, D), BF),
        pltpu.VMEM((4, TOK, D), BF),
        pltpu.VMEM((2, TOK, D), BF),
        pltpu.VMEM((1, TOK, D), BF),
    ]


class FoldR:
    def __init__(self, net, place, far, own, slots, order):
        one, two = order
        self.own, self.slots = own, slots
        self.both = net.add(lambda k: (far(3), slots.at[0], place.dev_r(one)))
        self.first = net.add(lambda k: (far(one), slots.at[1], place.dev_r(one)))
        self.second = net.add(lambda k: (slots.at[0], slots.at[2], place.dev_r(two)))

    def begin(self):
        self.both().start()
        self.first().start()

    def advance(self):
        self.both().wait_recv()
        add_rows(self.slots.at[0], self.own.at[1], self.slots.at[0])
        self.second().start()

    def gather(self):
        self.first().wait_recv()
        add_rows(self.slots.at[1], self.own.at[0], self.slots.at[1])

    def end(self, out=None):
        self.second().wait_recv()
        out = self.slots.at[2] if out is None else out
        add_rows(out, self.slots.at[1], self.slots.at[2])


def weight_folds(n, net, place, grads, own, slots):
    view = grads.reshape(4, n // 8, 2 * (D // n), grads.shape[-1])
    both = orders(2)
    halves, pieces = [], []
    for h in range(2):

        def piece(i, h=h):
            return view.at[pl.ds(2 * h, 2), place.rr_of(i)]

        halves.append(FoldR(net, place, piece, own.at[h], slots.at[h], both[h]))
        pieces.append((piece(0), own.at[h, 0]))
        pieces.append((piece(both[h][1]), own.at[h, 1]))
    return halves, pieces


def gradient_tiles(lhs, tiles, sem, products):
    wide = tiles.shape[-1]
    count = D // wide

    def fetch(f):
        cols = pl.ds(pl.multiple_of(f * wide, wide), wide)
        return pltpu.make_async_copy(lhs.at[:, :, cols], tiles.at[f % 2], sem.at[f % 2])

    def put(f, stage, out, sems):
        rows = pl.ds(pl.multiple_of(f * wide, wide), wide)
        return pltpu.make_async_copy(stage.at[f % 2], out.at[rows, :], sems.at[f % 2])

    fetch(0).start()

    def step(f, carry):
        fetch(f).wait()

        @pl.when(f + 1 < count)
        def _():
            fetch(f + 1).start()

        left = tiles[f % 2].reshape(8 * TOK, wide)
        for rhs, stage, out, sems in products:

            @pl.when(f >= 2)
            def _(stage=stage, out=out, sems=sems):
                put(f - 2, stage, out, sems).wait()

            right = rhs[...].reshape(8 * TOK, rhs.shape[-1])
            stage[f % 2] = contract_rows(left, right).astype(BF)
            put(f, stage, out, sems).start()
        return carry

    lax.fori_loop(0, count, step, 0)
    for f in (count - 2, count - 1):
        for _, stage, out, sems in products:
            put(f, stage, out, sems).wait()


def half_fold(net, place, grads, h, own, slots):
    order = orders(2)[h]
    cols = pl.ds(h * (FFT // 2), FFT // 2)

    def piece(i):
        return grads.at[:, place.rr_of(i), :, cols]

    fold = FoldR(net, place, piece, own, slots, order)
    return fold, [(piece(0), own.at[0]), (piece(order[1]), own.at[1])]


def return_one_kernel(
    n, dk, dv, o, z, w_out, w_down, gy, a2, dh,
    p_own, dk_own, dv_own, up_sum, g_out, g_down, g_up,
    zov, wdo, dhv, kown, vown, data, cs, zs, ys, ks, vs, tiles, st_wide, st_head, uown, us,
    send, recv, load, fetch_sem, put_sem, near,
):
    place = Place(n)
    net = Net(send, recv)
    greet(place, (1, 2, 4), (1, 2))
    both = orders(2)
    keys = FoldR(net, place, lambda i: dk.at[i], kown, ks, both[0])
    values = FoldR(net, place, lambda i: dv.at[i], vown, vs, both[1])
    total = FoldT(net, place, data, cs, zs, ys, p_own)
    up, pieces = half_fold(
        net, place, g_up.reshape(4, n // 8, 2 * (D // n), FFT), 0, uown, us
    )
    keys.both().start()
    values.both().start()

    loads = [
        pltpu.make_async_copy(src, dst, load.at[k])
        for k, (src, dst) in enumerate(
            (
                (z, zov.at[:, :, :FFT]),
                (o, zov.at[:, :, FFT:]),
                (w_down, wdo.at[:, :FFT]),
                (w_out, wdo.at[:, FFT:]),
                (dk.at[2], kown.at[1]),
                (dv.at[1], vown.at[1]),
                (dk.at[0], kown.at[0]),
                (dv.at[0], vown.at[0]),
                (dh, dhv),
            )
        )
    ]
    for copy in loads:
        copy.start()
    for copy in loads[:4]:
        copy.wait()

    def make(s, idx):
        del s, idx

    def emit(s, idx, put):
        put((slice(None), slice(None)), contract_cols(zov[s], wdo[...]))

    def after(idx):
        @pl.when(idx == 3)
        def _():
            keys.first().start()
            values.first().start()

        @pl.when(idx == 6)
        def _():
            for copy in loads[4:]:
                copy.wait()
            keys.advance()
            values.advance()

    total.loop(make, emit, after)
    total.turn_z1()
    gradient_tiles(a2, tiles, fetch_sem, [(dhv, st_wide, g_up, put_sem.at[0])])
    own_loads = [
        pltpu.make_async_copy(src, dst, near.at[k]) for k, (src, dst) in enumerate(pieces)
    ]
    up.begin()
    for copy in own_loads:
        copy.start()
    keys.gather()
    values.gather()
    gradient_tiles(
        gy, tiles, fetch_sem,
        [
            (zov.at[:, :, :FFT], st_wide, g_down, put_sem.at[0]),
            (zov.at[:, :, FFT:], st_head, g_out, put_sem.at[1]),
        ],
    )
    for copy in own_loads:
        copy.wait()
    up.advance()
    keys.end(dk_own)
    values.end(dv_own)
    total.turn_own()
    up.gather()
    up.end(up_sum)
    total.end()
    net.finish()


def return_one(n, dk, dv, o, z, w_out, w_down, gy, a2, dh):
    rows = 2 * (D // n)
    head, cols = (8, TOK, HEAD), (8, TOK, FFT)
    half = (4, rows, FFT // 2)
    outs = [
        jax.ShapeDtypeStruct((TOK, D), F32),
        jax.ShapeDtypeStruct(head, BF),
        jax.ShapeDtypeStruct(head, BF),
        jax.ShapeDtypeStruct(half, BF),
        jax.ShapeDtypeStruct((D, HEAD), BF),
        jax.ShapeDtypeStruct((D, FFT), BF),
        jax.ShapeDtypeStruct((D, FFT), BF),
    ]
    scratch = [
        pltpu.VMEM((8, TOK, FFT + HEAD), BF),
        pltpu.VMEM((D, FFT + HEAD), BF),
        pltpu.VMEM(cols, BF),
        pltpu.VMEM((2, *head), BF),
        pltpu.VMEM((2, *head), BF),
        *fold_scratch(),
        pltpu.VMEM((3, *head), BF),
        pltpu.VMEM((3, *head), BF),
        pltpu.VMEM((2, 8, TOK, WIDE), BF),
        pltpu.VMEM((2, WIDE, FFT), BF),
        pltpu.VMEM((2, WIDE, HEAD), BF),
        pltpu.VMEM((2, *half), BF),
        pltpu.VMEM((3, *half), BF),
    ]

    def kernel(*refs):
        return_one_kernel(n, *refs)

    return pl.pallas_call(
        kernel,
        out_shape=outs,
        in_specs=[ANY] * 9,
        out_specs=[VM] * 4 + [ANY] * 3,
        scratch_shapes=[
            *scratch,
            pltpu.SemaphoreType.DMA((16,)),
            pltpu.SemaphoreType.DMA((16,)),
            pltpu.SemaphoreType.DMA((9,)),
            pltpu.SemaphoreType.DMA((2,)),
            pltpu.SemaphoreType.DMA((2, 2)),
            pltpu.SemaphoreType.DMA((2,)),
        ],
        compiler_params=pltpu.CompilerParams(
            collective_id=2, has_side_effects=True, vmem_limit_bytes=62 * MIB
        ),
    )(dk, dv, o, z, w_out, w_down, gy, a2, dh)


def return_two_kernel(
    n, gi, gu0, gu, go, gd, dq, dk, dv, a1, x, dh, w_in, w_up, cosine, sine, smt, stats, sums,
    oi, ou, oo, od, e_own, osmall, gi_out,
    dqv, dkv, dvv, djp, djn, dhv, wi, wu, xt, cst, snt, data, cs, zs, ys, tile, other,
    uown, us, ui, uo, ud, si, so, sd, term, blocks, sslots, tiles, st_in,
    send, recv, load, near, x_sem, fetch_sem, put_sem, last_sem,
):
    del gi
    place = Place(n)
    net = Net(send, recv)
    rb = D // n
    R = place.R
    both = orders(2)
    greet(place, range(1, 8), (1, 2))
    names = ((gd, ud, sd, od, 3), (go, uo, so, oo, 2), (gi_out, ui, si, oi, 0))
    parts, pieces = [], []
    for src, own, slots, _, _ in names:
        halves, near_pieces = weight_folds(n, net, place, src, own, slots)
        parts.append(halves)
        pieces += near_pieces
    small = FoldR(
        net, place, lambda i: blocks.at[place.rr_of(i)], None, sslots, both[0]
    )
    total = FoldT(net, place, data, cs, zs, ys, e_own)
    up, up_pieces = half_fold(net, place, gu.reshape(4, R, 2 * rb, FFT), 1, uown, us)

    finals = []
    ends = []
    for _, _, slots, dst, k in names:
        count, width = WEIGHTS[k]
        ends.append(
            (
                lambda zt, rows, cols, slots=slots: slots.at[zt // 2, 2, zt % 2, rows, cols],
                dst, width, [(p * width, p * D) for p in range(count)],
            )
        )
    for h in range(2):
        summed = us.at[2] if h else gu0
        ends.append(
            (
                lambda zt, rows, cols, summed=summed: summed.at[zt, rows, cols],
                ou, FFT // 2, [(0, h * (FFT // 2))],
            )
        )
    for which, (summed, dst, width, spans) in enumerate(ends):
        stride = FFT if dst is ou else width
        ops = []
        for s in range(8):
            rows = pl.ds(pl.multiple_of(place.c_of(s) * rb, rb), rb)
            for p, (at, into) in enumerate(spans):
                cols = pl.ds(pl.multiple_of(into + place.t * stride, 128), width)
                piece = summed(place.zt_of(s), rows, pl.ds(at, width))
                if s == 0:
                    ops.append(
                        pltpu.make_async_copy(
                            piece, dst.at[:, cols], last_sem.at[which * 3 + p]
                        )
                    )
                else:
                    ops.append(
                        net.add(
                            lambda k, piece=piece, dst=dst, cols=cols, s=s: (
                                piece, dst.at[:, cols], place.dev_t(s),
                            )
                        )
                    )
        finals.append(ops)
    small_last = [
        net.add(
            lambda k, s=s: (
                sslots.at[2, place.zt_of(s)], osmall.at[place.t], place.dev_t(s),
            )
        )
        for s in range(1, 8)
    ]
    small_mine = pltpu.make_async_copy(
        sslots.at[2, place.zt], osmall.at[place.t], last_sem.at[15]
    )

    def send_finals(which):
        for k, op in enumerate(finals[which]):
            (op if k < len(ends[which][3]) else op()).start()

    def wait_finals(which):
        for k, op in enumerate(finals[which]):
            if k < len(ends[which][3]):
                op.wait()
            else:
                op().wait_recv()

    up.begin()
    send_finals(3)
    loads = [
        pltpu.make_async_copy(src, dst, load.at[k])
        for k, (src, dst) in enumerate(
            (
                (dq, dqv), (dk, dkv), (dv, dvv), (cosine, cst), (sine, snt),
                (w_in, wi), (dh, dhv), (w_up, wu),
            )
        )
    ]
    for copy in loads:
        copy.start()
    own_loads = [
        pltpu.make_async_copy(src, dst, near.at[k])
        for k, (src, dst) in enumerate(pieces + up_pieces)
    ]
    for copy in own_loads[:8] + own_loads[12:]:
        copy.start()

    def fetch_x(s, slot):
        return pltpu.make_async_copy(x.at[s], xt.at[slot], x_sem.at[slot])

    fetch_x(7, 0).start()
    term[...] = sums[...]
    shuffle = shuffle_matrix().astype(BF)
    head_cols = pl.ds(pl.multiple_of(place.t * HEAD, HEAD), HEAD)
    for copy in loads:
        copy.wait()
    chunk_cols = 256

    def joint(s):
        csn, sn = cst[s], snt[s]
        half = HEAD // 2
        for p, src in enumerate((dqv, dkv)):
            one = src[s, :, :half].astype(F32)
            two = src[s, :, half:].astype(F32)
            cols = slice(p * HEAD, (p + 1) * HEAD)
            djp[:, p * HEAD : p * HEAD + half] = (one * csn + two * sn).astype(BF)
            djp[:, p * HEAD + half : (p + 1) * HEAD] = (two * csn - one * sn).astype(BF)
            natural = contract_cols(djp[:, cols], shuffle)
            djn[s, :, cols] = natural.astype(BF)
            term[4 + p : 5 + p, head_cols] += jnp.sum(natural, axis=0, keepdims=True)
        value = dvv[s]
        djp[:, 2 * HEAD :] = value
        djn[s, :, 2 * HEAD :] = value
        term[6:7, head_cols] += jnp.sum(value.astype(F32), axis=0, keepdims=True)

    def make(s, idx):
        joint(s)
        fetch_x(s, idx % 2).wait()

        @pl.when(idx < 7)
        def _():
            fetch_x(total.order(idx + 1), (idx + 1) % 2).start()

        tile[...] = contract_cols(djp[...], wi[...])
        other[...] = contract_cols(dhv[s], wu[...])

    def emit(s, idx, put):
        average = stats[s, :, 0:1]
        inverse = stats[s, :, 1:2]

        def chunk(k, carry):
            cols = pl.ds(pl.multiple_of(k * chunk_cols, chunk_cols), chunk_cols)
            xhat = (xt[idx % 2, :, cols].astype(F32) - average) * inverse
            one, two = tile[:, cols], other[:, cols]
            for row, value in ((0, one * xhat), (1, one), (2, two * xhat), (3, two)):
                term[row : row + 1, cols] += jnp.sum(value, axis=0, keepdims=True)
            put((slice(None), cols), one * smt[0:1, cols] + two * smt[2:3, cols])
            return carry

        lax.fori_loop(0, D // chunk_cols, chunk, 0)

    def after(idx):
        @pl.when(idx == 1)
        def _():
            for part in parts[0]:
                part.begin()

        @pl.when(idx == 3)
        def _():
            for copy in own_loads[12:]:
                copy.wait()
            up.advance()

        @pl.when(idx == 4)
        def _():
            for part in parts[1]:
                part.begin()

        @pl.when(idx == 5)
        def _():
            up.gather()
            up.end()
            send_finals(4)

        @pl.when(idx == 6)
        def _():
            for copy in own_loads[:4]:
                copy.wait()
            for part in parts[0]:
                part.advance()
            total.turn_z1()

    total.loop(make, emit, after)

    for rr in range(R):
        for zt in range(4):
            at = (zt * R + rr) * 128
            blocks[rr, zt] = term[:, at : at + 128]
    small.both().start()
    small.first().start()
    gradient_tiles(a1, tiles, fetch_sem, [(djn, st_in, gi_out, put_sem)])
    for part in parts[2]:
        part.begin()
    for copy in own_loads[8:12]:
        copy.start()
    for part in parts[0]:
        part.gather()
        part.end()
    send_finals(0)
    for copy in own_loads[4:8]:
        copy.wait()
    for part in parts[1]:
        part.advance()
    total.turn_own()
    small.both().wait_recv()
    sslots[0] = sslots[0] + blocks[place.rr_of(2)]
    small.second().start()
    for copy in own_loads[8:12]:
        copy.wait()
    for part in parts[2]:
        part.advance()
    for part in parts[1]:
        part.gather()
        part.end()
    send_finals(1)
    small.first().wait_recv()
    small.second().wait_recv()
    sslots[2] = sslots[2] + (sslots[1] + blocks[place.rr])
    small_mine.start()
    for op in small_last:
        op().start()
    for part in parts[2]:
        part.gather()
        part.end()
    send_finals(2)
    total.end()
    for which in range(5):
        wait_finals(which)
    small_mine.wait()
    for op in small_last:
        op().wait_recv()
    net.finish()


def return_two(n, up_sum, g_up, g_out, g_down, dq, dk, dv, a1, x, dh, w_in, w_up, cosine, sine, smt, stats, sums):
    rb = D // n
    R = n // 8
    head, cols, block = (8, TOK, HEAD), (8, TOK, FFT), (8, TOK, D)
    outs = [jax.ShapeDtypeStruct((rb, HEADS * parts * width), BF) for parts, width in WEIGHTS]
    outs += [
        jax.ShapeDtypeStruct((TOK, D), F32),
        jax.ShapeDtypeStruct((8, SMALLR, 128), F32),
        jax.ShapeDtypeStruct((D, 3 * HEAD), BF),
    ]
    wide = [parts * width for parts, width in WEIGHTS]
    scratch = [
        pltpu.VMEM(head, F32),
        pltpu.VMEM(head, BF),
        pltpu.VMEM(head, BF),
        pltpu.VMEM((TOK, 3 * HEAD), BF),
        pltpu.VMEM((8, TOK, 3 * HEAD), BF),
        pltpu.VMEM(cols, BF),
        pltpu.VMEM((D, 3 * HEAD), BF),
        pltpu.VMEM((D, FFT), BF),
        pltpu.VMEM((2, TOK, D), BF),
        pltpu.VMEM((8, TOK, HEAD // 2), F32),
        pltpu.VMEM((8, TOK, HEAD // 2), F32),
        *fold_scratch(),
        pltpu.VMEM((TOK, D), F32),
        pltpu.VMEM((TOK, D), F32),
        pltpu.VMEM((2, 4, 2 * rb, FFT // 2), BF),
        pltpu.VMEM((3, 4, 2 * rb, FFT // 2), BF),
        *[pltpu.VMEM((2, 2, 2, 2 * rb, wide[k]), BF) for k in (0, 2, 3)],
        *[pltpu.VMEM((2, 3, 2, 2 * rb, wide[k]), BF) for k in (0, 2, 3)],
        pltpu.VMEM((SMALLR, D), F32),
        pltpu.VMEM((R, 4, SMALLR, 128), F32),
        pltpu.VMEM((3, 4, SMALLR, 128), F32),
        pltpu.VMEM((2, 8, TOK, HEAD), BF),
        pltpu.VMEM((2, HEAD, 3 * HEAD), BF),
    ]
    copies = 6 * 3 + 3 + 3 + 7 + 7 * 7 + 7

    def kernel(*refs):
        return_two_kernel(n, None, *refs)

    return pl.pallas_call(
        kernel,
        out_shape=outs,
        in_specs=[ANY] * 14 + [VM] * 3,
        out_specs=[ANY] * 4 + [VM] + [ANY] * 2,
        scratch_shapes=[
            *scratch,
            pltpu.SemaphoreType.DMA((copies,)),
            pltpu.SemaphoreType.DMA((copies,)),
            pltpu.SemaphoreType.DMA((8,)),
            pltpu.SemaphoreType.DMA((16,)),
            pltpu.SemaphoreType.DMA((2,)),
            pltpu.SemaphoreType.DMA((2,)),
            pltpu.SemaphoreType.DMA((2,)),
            pltpu.SemaphoreType.DMA((16,)),
        ],
        compiler_params=pltpu.CompilerParams(
            collective_id=3, has_side_effects=True, vmem_limit_bytes=62 * MIB
        ),
    )(up_sum, g_up, g_out, g_down, dq, dk, dv, a1, x, dh, w_in, w_up, cosine, sine, smt, stats, sums)


def token_row(base, core, size=RUN):
    lane = lax.broadcasted_iota(jnp.int32, (1, size), 1)
    return base + (lane + core * TOK) % RUN


def token_col(base, core, size=RUN):
    row = lax.broadcasted_iota(jnp.int32, (size, 1), 0)
    return base + (row + core * TOK) % RUN


def start_of(tokens, lengths, nseq):
    out, begin = tokens * 0, lengths[0] * 0
    for s in range(nseq):
        out = jnp.where(tokens >= begin, begin, out)
        begin = begin + lengths[s]
    return out


def run_facts(place, lengths, nseq, u):
    number = place.zt_of_run(u) * place.R + place.rr
    count = number - start_of(number * RUN, lengths, nseq) // RUN + 1
    return number, count, start_of(number * RUN + RUN - 1, lengths, nseq)


def scores_of(key, query):
    return lax.dot_general(key, query, (((1,), (1,)), ((), ())), preferred_element_type=F32)


def seen_mask(core, gq, gk, lengths, nseq):
    tq = token_row(gq * RUN, core)
    tk = token_col(gk * RUN, core)
    return (tk <= tq) & (tk >= start_of(tq, lengths, nseq))


def attend_kernel(
    n, nseq, lengths, q, dout, kg, vg, o, stats, m, l, acc, kv, sem
):
    u = pl.program_id(0)
    place = Place(n)
    number, count, last = run_facts(place, lengths, nseq, u)
    m[...] = jnp.full_like(m, NEGATIVE)
    l[...] = jnp.zeros_like(l)
    acc[...] = jnp.zeros_like(acc)

    def fetch(d, slot):
        far = number - d
        moved = (far // place.R) ^ place.zt
        i, ku = (far % place.R) ^ place.rr, moved % 2 * 2 + moved // 2
        return [
            pltpu.make_async_copy(src.at[i, :, ku], kv.at[slot, p], sem.at[slot, p])
            for p, src in enumerate((kg, vg))
        ]

    def block(slot, far, masked):
        query = q[...].reshape(RUN, HEAD)
        key = kv[slot, 0].reshape(RUN, HEAD)
        value = kv[slot, 1].reshape(RUN, HEAD)
        s = scores_of(key, query)
        if masked:
            s = jnp.where(seen_mask(place.c, number, number - far, lengths, nseq), s, NEGATIVE)
        old = m[0:1, :]
        new = jnp.maximum(old, jnp.max(s, axis=0, keepdims=True))
        p = jnp.exp(s - new)
        fade = jnp.exp(old - new)
        l[0:1, :] = l[0:1, :] * fade + jnp.sum(p, axis=0, keepdims=True)
        m[0:1, :] = new
        mixed = lax.dot_general(
            value, p.astype(BF), (((0,), (0,)), ((), ())), preferred_element_type=F32
        )
        acc[...] = acc[...] * fade + mixed

    for copy in fetch(0, 0):
        copy.start()

    def step(d, carry):
        slot = d % 2
        for copy in fetch(d, slot):
            copy.wait()

        @pl.when(d + 1 < count)
        def _():
            for copy in fetch(d + 1, 1 - slot):
                copy.start()

        edge = (d == 0) | ((number - d) * RUN < last)

        @pl.when(edge)
        def _():
            block(slot, d, True)

        @pl.when(jnp.logical_not(edge))
        def _():
            block(slot, d, False)

        return carry

    lax.fori_loop(0, count, step, 0)
    out = acc[...] / l[0:1, :]
    rows = out.T
    o[...] = rows.astype(BF).reshape(o.shape)
    grad = dout[...].reshape(RUN, HEAD).astype(F32).T
    stats[0, 0:1, :] = m[0:1, :] + jnp.log(l[0:1, :])
    stats[0, 1:2, :] = jnp.sum(out * grad, axis=0, keepdims=True)
    stats[0, 2:8, :] = jnp.zeros((6, RUN), F32)


def attend(n, lengths, q, dout, kg, vg):
    run = pl.BlockSpec((2, 1, TOK, HEAD), lambda u, *_: (0, u, 0, 0))

    def kernel(*refs):
        attend_kernel(n, lengths.shape[0], *refs)

    return pl.pallas_call(
        kernel,
        out_shape=[
            jax.ShapeDtypeStruct((2, 4, TOK, HEAD), BF),
            jax.ShapeDtypeStruct((4, 8, RUN), F32),
        ],
        grid_spec=pltpu.PrefetchScalarGridSpec(
            num_scalar_prefetch=1,
            grid=(4,),
            in_specs=[run, run, ANY, ANY],
            out_specs=[run, pl.BlockSpec((1, 8, RUN), lambda u, *_: (u, 0, 0))],
            scratch_shapes=[
                pltpu.VMEM((8, RUN), F32),
                pltpu.VMEM((8, RUN), F32),
                pltpu.VMEM((HEAD, RUN), F32),
                pltpu.VMEM((2, 2, 2, TOK, HEAD), BF),
                pltpu.SemaphoreType.DMA((2, 2)),
            ],
        ),
        compiler_params=pltpu.CompilerParams(vmem_limit_bytes=62 * MIB),
        cost_estimate=pl.CostEstimate(
            flops=4 * 16 * RUN * RUN * HEAD, bytes_accessed=12 * MIB, transcendentals=16 * RUN * RUN
        ),
    )(lengths, q, dout, kg, vg)


def attend_back_kernel(
    n, nseq, lengths, q, dout, stats, k, v, dq, dk, dv, tq, tk, tv, facts
):
    block_at = pl.program_id(0)
    steps = pl.num_programs(0)

    place = Place(n)

    @pl.when(block_at == 0)
    def _():
        tq[...] = jnp.zeros_like(tq)
        for u in range(4):
            for f, value in enumerate(run_facts(place, lengths, nseq, u)):
                facts[4 * f + u] = value

    tk[...] = jnp.zeros_like(tk)
    tv[...] = jnp.zeros_like(tv)
    here = place.zt_of_run(block_at % 4) * place.R + (place.rr ^ (block_at // 4))

    for u in range(4):
        far = facts[u] - here
        active = (far >= 0) & (far < facts[4 + u])
        edge = (far == 0) | (here * RUN < facts[8 + u])

        def block(masked, u=u):
            query = q[:, u].reshape(RUN, HEAD)
            grad = dout[:, u].reshape(RUN, HEAD)
            key = k[...].reshape(RUN, HEAD)
            value = v[...].reshape(RUN, HEAD)
            s = scores_of(key, query)
            p = jnp.exp(s - stats[u, 0:1, :])
            if masked:
                p = jnp.where(seen_mask(place.c, facts[u], here, lengths, nseq), p, 0.0)
            dp = scores_of(value, grad)
            ds = (p * (dp - stats[u, 1:2, :])).astype(BF)
            tv[...] += jnp.dot(p.astype(BF), grad, preferred_element_type=F32)
            tk[...] += jnp.dot(ds, query, preferred_element_type=F32)
            tq[u] += lax.dot_general(
                ds, key, (((0,), (0,)), ((), ())), preferred_element_type=F32
            )

        @pl.when(active & edge)
        def _(block=block):
            block(True)

        @pl.when(active & jnp.logical_not(edge))
        def _(block=block):
            block(False)

    dk[...] = tk[...].astype(BF).reshape(dk.shape)
    dv[...] = tv[...].astype(BF).reshape(dv.shape)

    @pl.when(block_at == steps - 1)
    def _():
        for u in range(4):
            dq[:, u] = (tq[u] * HEAD**-0.5).reshape(2, TOK, HEAD)


def attend_back(n, lengths, q, dout, stats, kg, vg):
    R = n // 8
    whole = pl.BlockSpec((2, 4, TOK, HEAD), lambda b, *_: (0, 0, 0, 0))
    key = pl.BlockSpec((1, 2, 1, TOK, HEAD), lambda b, *_: (b // 4, 0, b % 4, 0, 0))

    def kernel(*refs):
        attend_back_kernel(n, lengths.shape[0], *refs)

    return pl.pallas_call(
        kernel,
        out_shape=[
            jax.ShapeDtypeStruct((2, 4, TOK, HEAD), F32),
            jax.ShapeDtypeStruct((R, 2, 4, TOK, HEAD), BF),
            jax.ShapeDtypeStruct((R, 2, 4, TOK, HEAD), BF),
        ],
        grid_spec=pltpu.PrefetchScalarGridSpec(
            num_scalar_prefetch=1,
            grid=(4 * R,),
            in_specs=[
                whole,
                whole,
                pl.BlockSpec((4, 8, RUN), lambda b, *_: (0, 0, 0)),
                key,
                key,
            ],
            out_specs=[whole, key, key],
            scratch_shapes=[
                pltpu.VMEM((4, RUN, HEAD), F32),
                pltpu.VMEM((RUN, HEAD), F32),
                pltpu.VMEM((RUN, HEAD), F32),
                pltpu.SMEM((12,), jnp.int32),
            ],
        ),
        compiler_params=pltpu.CompilerParams(vmem_limit_bytes=62 * MIB),
        cost_estimate=pl.CostEstimate(
            flops=10 * 16 * RUN * RUN * HEAD, bytes_accessed=24 * MIB, transcendentals=16 * RUN * RUN
        ),
    )(lengths, q, dout, stats, kg, vg)


def adam_step(parameter, gradient, first_moment, second_moment, step_rate):
    first_new = BETA_ONE * first_moment + (1.0 - BETA_ONE) * gradient
    second_new = BETA_TWO * second_moment + (1.0 - BETA_TWO) * gradient * gradient
    first_hat = first_new / (1.0 - BETA_ONE**STEPS)
    second_hat = second_new / (1.0 - BETA_TWO**STEPS)
    parameter_new = parameter - step_rate * (
        first_hat / (jnp.sqrt(second_hat) + ADAM_EPS) + WEIGHT_DECAY * parameter
    )
    return (first_new, second_new, parameter_new)


def adam_kernel(rates, *refs):
    count = len(rates)
    x, gy, e, part, small = refs[:5]
    groups = [refs[5 + k * count : 5 + (k + 1) * count] for k in range(7)]
    block_out, token_grad = refs[5 + 7 * count :]
    for p, g, m, v, rate, p_out, m_out, v_out in zip(
        *groups[:4], rates, *groups[4:]
    ):
        m_out[...], v_out[...], p_out[...] = adam_step(
            p[...], g[...].astype(F32), m[...], v[...], rate
        )
    xf, grad = x[...].astype(F32), e[...]
    block_out[...] = (xf + part[...] + small[7:8, :] + small[8:9, :]).astype(BF)
    centred = xf - jnp.mean(xf, axis=-1, keepdims=True)
    inverse = lax.rsqrt(jnp.mean(centred * centred, axis=-1, keepdims=True) + NORM_EPS)
    xhat = centred * inverse
    token_grad[...] = gy[...].astype(F32) + inverse * (
        grad
        - jnp.mean(grad, axis=-1, keepdims=True)
        - xhat * jnp.mean(grad * xhat, axis=-1, keepdims=True)
    )


def adam(own, params, grads, firsts, seconds, rates):
    steps = 8

    def spec(a):
        return pl.BlockSpec((a.shape[0], a.shape[1] // steps), lambda k: (0, k))

    tok = pl.BlockSpec((TOK // steps, D), lambda k: (k, 0))
    small = pl.BlockSpec((SMALLR, D), lambda k: (0, 0))
    arrays = [*params, *grads, *firsts, *seconds]
    outs = [jax.ShapeDtypeStruct(p.shape, F32) for _ in range(3) for p in params]
    own_outs = [jax.ShapeDtypeStruct((TOK, D), BF), jax.ShapeDtypeStruct((TOK, D), F32)]

    def kernel(*refs):
        adam_kernel(rates, *refs)

    out = pl.pallas_call(
        kernel,
        out_shape=[*outs, *own_outs],
        grid=(steps,),
        in_specs=[tok] * 4 + [small] + [spec(a) for a in arrays],
        out_specs=[spec(a) for a in outs] + [tok] * 2,
        compiler_params=pltpu.CompilerParams(vmem_limit_bytes=62 * MIB),
    )(*own, *arrays)
    count = len(params)
    return [out[k * count : (k + 1) * count] for k in range(3)] + list(out[3 * count :])


def contract_rows(left, right):
    return lax.dot_general(left, right, (((0,), (0,)), ((), ())), preferred_element_type=F32)


def contract_cols(left, right):
    return lax.dot_general(left, right, (((1,), (1,)), ((), ())), preferred_element_type=F32)


def paired(columns):
    turned, half = HEAD // 8, HEAD // 2
    heads = columns.reshape(columns.shape[0], -1, HEAD)
    cut = 2 * turned + half - turned
    order = [(0, turned), (2 * turned, cut), (turned, 2 * turned), (cut, HEAD)]
    return jnp.concatenate([heads[..., a:b] for a, b in order], axis=-1).reshape(columns.shape)


def unpaired(columns):
    turned, half = HEAD // 8, HEAD // 2
    heads = columns.reshape(columns.shape[0], -1, HEAD)
    order = [(0, turned), (half, half + turned), (turned, half), (half + turned, HEAD)]
    return jnp.concatenate([heads[..., a:b] for a, b in order], axis=-1).reshape(columns.shape)


def turn(values, cosine, sine):
    half = HEAD // 2
    one, two = values[:, :half], values[:, half:]
    return jnp.concatenate([one * cosine - two * sine, two * cosine + one * sine], axis=1)


def pack_small(columns, n):
    rb = D // n
    blocks = columns.reshape(SMALLR, n, rb).transpose(1, 0, 2)
    return jnp.pad(blocks, ((0, 0), (0, 0), (0, 128 - rb)))


def return_plain(n, gg, xg, a1, a2, z, dh, o, dq, dk, dv, ws, cosine, sine, small_all, sums):
    place = Place(n)
    R, rb, rows = n // 8, D // n, 8 * TOK
    a1, a2, gy, z, dh, o, dq = (v.reshape(rows, -1) for v in (a1, a2, gg, z, dh, o, dq))
    w_in, w_up, w_out, w_down = (g.reshape(D, -1) for g in ws)
    cosine, sine = cosine.reshape(rows, -1), sine.reshape(rows, -1)
    g1, g2 = small_all[0], small_all[2]
    xf = xg.reshape(rows, D).astype(F32)
    centred = xf - jnp.mean(xf, axis=-1, keepdims=True)
    xhat = centred * lax.rsqrt(jnp.mean(centred * centred, axis=-1, keepdims=True) + NORM_EPS)
    partial_out = (contract_cols(o, w_out) + contract_cols(z, w_down)).astype(BF)
    ins = {"k": dk, "v": dv, "p": partial_out.reshape(8, TOK, D)}
    back = {}
    for at, name in enumerate(ins):
        back |= return_keys(n, {name: ins[name]}, 4 + at)
    dq = turn(dq, cosine, -sine)
    dk = turn(back["k"].reshape(rows, HEAD).astype(F32), cosine, -sine)
    dj = jnp.concatenate([dq.astype(BF), dk.astype(BF), back["v"].reshape(rows, HEAD)], axis=1)
    da1 = contract_cols(dj, w_in)
    da2 = contract_cols(dh, w_up)
    e = (da1 * g1 + da2 * g2).astype(BF)
    norm_grads = [jnp.sum(v, axis=0) for v in (da1 * xhat, da1, da2 * xhat, da2)]
    dj = jnp.concatenate([unpaired(dj[:, : 2 * HEAD]), dj[:, 2 * HEAD :]], axis=1)
    dj_sum = jnp.sum(dj.astype(F32), axis=0).reshape(3, HEAD)
    own_cols = lax.dynamic_update_slice(
        jnp.zeros((SMALLR, D), F32), dj_sum, (jnp.int32(4), place.t * HEAD)
    )
    small_term = own_cols + sums
    small_term = small_term.at[:4].set(jnp.stack(norm_grads))
    small_blocks = pack_small(small_term, n).reshape(4, R, 2 * SMALLR, 128)
    grads = [
        contract_rows(left, right).astype(BF).reshape(4, R, 2 * rb, -1)
        for left, right in ((a1, dj), (a2, dh), (gy, o), (gy, z))
    ]
    *weight_grads, e_own, small_parts = return_grads(
        n, grads, e.reshape(8, TOK, D), small_blocks, 3
    )
    return back["p"], weight_grads, e_own, jnp.sum(small_parts, axis=0)[:SMALLC, :rb].T


def body(
    tokens, cotangent, lengths,
    attend_in, widening, attend_out, narrowing, small_params,
    first_attend_in, first_widening, first_attend_out, first_narrowing, first_small,
    second_attend_in, second_widening, second_attend_out, second_narrowing, second_small,
):
    n = lax.axis_size("fsdp")
    place = Place(n)
    R = place.R
    rb = D // n
    turned = HEAD // 8
    lanes = jnp.arange(HEAD // 2, dtype=jnp.int32)
    frequency = jnp.where(
        lanes < turned, ROPE_BASE ** (-2.0 * lanes.astype(F32) / (2 * turned)), 0.0
    )[None, :]

    small_rows = jnp.pad(small_params, ((0, 0), (0, 128 - SMALLC)))
    low_in = attend_in.astype(BF)
    low_in = jnp.concatenate([paired(low_in[:, : 2 * D]), low_in[:, 2 * D :]], axis=1)
    weights = [low_in] + [w.astype(BF) for w in (widening, attend_out, narrowing)]
    runs = (2, 4, TOK, HEAD)
    xg, gg, a1, a2, *ws, q, kg, vg, z, dh, dout, small_all, sums, stats_x, cosine, sine = forward(
        n, tokens, cotangent, weights, small_rows, lengths, frequency
    )
    xg, gg, a1, a2, z, dh, stats_x, cosine, sine = (
        v.reshape(8, TOK, v.shape[-1]) for v in (xg, gg, a1, a2, z, dh, stats_x, cosine, sine)
    )

    kg = kg.reshape(R, *runs)
    vg = vg.reshape(R, *runs)
    q4, dout4 = q.reshape(runs), dout.reshape(runs)
    o4, stats = attend(n, lengths, q4, dout4, kg, vg)
    dq4, dk5, dv5 = attend_back(n, lengths, q4, dout4, stats, kg, vg)
    o, dq = o4.reshape(8, TOK, HEAD), dq4.reshape(8, TOK, HEAD)
    dk, dv = dk5.reshape(R, 8, TOK, HEAD), dv5.reshape(R, 8, TOK, HEAD)
    if R == 4:
        p_own, dk, dv, up_sum, g_out, g_down, g_up = return_one(
            n, dk, dv, o, z, ws[2].reshape(D, -1), ws[3].reshape(D, -1), gg, a2, dh
        )
        *weight_grads, e_own, small_parts, _ = return_two(
            n, up_sum, g_up, g_out, g_down, dq, dk, dv, a1, xg, dh,
            ws[0].reshape(D, -1), ws[1].reshape(D, -1), cosine, sine, small_all, stats_x, sums,
        )
        own_lanes = lax.dynamic_slice(
            jnp.sum(small_parts, axis=0), (0, place.c * rb), (SMALLR, rb)
        )
        small_grad = own_lanes[:SMALLC].T
    else:
        p_own, weight_grads, e_own, small_grad = return_plain(
            n, gg, xg, a1, a2, z, dh, o, dq, dk, dv, ws, cosine, sine, small_all, sums
        )
    gr_in, gr_up, gr_out, gr_down = weight_grads
    rate_inner = 2.5 * D ** (-0.5)
    rate_outer = 2.5 * (D * 11 // LMAX) ** (-0.5)
    rate_down = 2.5 * FF ** (-0.5)
    rate_small = 0.5
    new, mean, square, block_out, token_grad = adam(
        (tokens, cotangent, e_own, p_own, small_all),
        (attend_in, widening, attend_out, narrowing),
        (gr_in, gr_up, gr_out, gr_down),
        (first_attend_in, first_widening, first_attend_out, first_narrowing),
        (second_attend_in, second_widening, second_attend_out, second_narrowing),
        (rate_inner, rate_inner, rate_outer, rate_down),
    )
    mean_small, square_small, new_small = adam_step(
        small_params, small_grad, first_small, second_small, rate_small
    )
    return (
        block_out,
        token_grad,
        *new,
        new_small,
        *mean,
        mean_small,
        *square,
        square_small,
    )


def solution(mesh):
    spec = P("fsdp", None)
    return jax.shard_map(
        body,
        mesh=mesh,
        in_specs=(spec, spec, P(), *[spec] * 15),
        out_specs=(spec,) * 17,
        check_vma=False,
    )
```

time: 3810 us -> 572 us (0.15)
  waiting for transfers between devices: 2030 us -> 0 us
  Pallas kernels: 0 us -> 563 us
  starting transfers between devices: 547 us -> 0 us
  matrix products: 390 us -> 0 us
  other arithmetic: 367 us -> 6.89 us
  local copies, waits for them, and re-layouts: 357 us -> 1.53 us
  loops' own time: 48.5 us -> 0 us
  blocking collectives: 44.6 us -> 0 us
    reduce_scatter x1 -> x0, waiting for transfers between devices: 1620 us -> none  [body(): lax.psum_scatter(jnp.concatenate([contract_rows(cols_one, grad_joint), co...]
    pallas_call x0 -> x6, Pallas kernels: none -> 563 us  [the longest x1 229 us: forward(): pl.pallas_call(kernel, out_shape=outs, in_specs=[ANY] * 7 + [pl.BlockSpec...]
    ppermute x32 -> x0, starting transfers between devices: 547 us -> none  [shifted(): return lax.ppermute(value, axis, pairs)]
    dot_general x113 -> x0, matrix products: 390 us -> none  [the longest x4 80.3 us: contract_rows(): lax.dot_general(left, right, (((0,), (0,)), ((), ())), preferred_element_...]
    all_gather x4 -> x0, waiting for transfers between devices: 169 us -> none  [the longest x1 148 us: body(): lax.all_gather(inner_low, 'fsdp', axis=0, tiled=True)]
    ppermute x32 -> x0, waiting for transfers between devices: 163 us -> none  [shifted(): return lax.ppermute(value, axis, pairs)]
    concatenate x3 -> x2, other arithmetic: 156 us -> 1.28 us  [the longest x1 0.93 us: body(): jnp.concatenate([paired(low_in[:, :2 * D]), low_in[:, 2 * D:]], axis=1)]
    dynamic_slice x101 -> x0, local copies, waits for them, and re-layouts: 121 us -> none  [the longest x34 48.2 us: block_grads(): lax.dynamic_index_in_dim(values_back, block_index, 0, keepdims=False)]
  transfers between devices with their start and end apart: 38 -> 0, of which waited for: 36 -> 0; matrix products, arithmetic and copies ran while one was open for 25% -> 0% of each run, Pallas kernels for 0% -> 0%
where the time goes in v1:
time: 572 us
  Pallas kernels  563 us (98%)
  other arithmetic  6.89 us (1%)
    pallas_call x1, Pallas kernels, forward(): pl.pallas_call(kernel, out_shape=outs, in_specs=[ANY] * 7 + [pl.BlockSpec...  229 us
    pallas_call x1, Pallas kernels, return_two(): pl.pallas_call(kernel, out_shape=outs, in_specs=[ANY] * 14 + [VM] * 3, ou...  160 us
    pallas_call x1, Pallas kernels, return_one(): pl.pallas_call(kernel, out_shape=outs, in_specs=[ANY] * 9, out_specs=[VM]...  107 us
    pallas_call x1, Pallas kernels, attend_back(): pl.pallas_call(kernel, out_shape=[jax.ShapeDtypeStruct((2, 4, TOK, HEAD),...  25.2 us
    pallas_call x1, Pallas kernels, attend(): pl.pallas_call(kernel, out_shape=[jax.ShapeDtypeStruct((2, 4, TOK, HEAD),...  22.1 us
    pallas_call x1, Pallas kernels, adam(): pl.pallas_call(kernel, out_shape=[*outs, *own_outs], grid=(steps,), in_sp...  20.1 us

profile of v1, /device:TPU:0, one launch (start us, length us, event | category | flops | bytes accessed | tf_op | source)
XLA Modules:
  0.0 572.4 jit_solution(5359150084248645947)
XLA Ops:
  0.7 1.5 convert_element_type.24
  2.2 0.1 copy.36
  2.3 0.1 fusion.4
  2.4 0.2 fusion.5
  2.7 0.0 copy-start
  2.7 0.3 pad_maximum_fusion.1
  3.0 0.2 copy.37
  3.3 0.9 pad_maximum_fusion.refs_2_
  4.2 0.1 copy-done
  4.3 1.1 convert_element_type.25.refs_3_
  5.3 1.1 convert_element_type.27.refs_5_
  6.4 0.0 copy-done.2
  6.4 0.7 convert_element_type.26.refs_4_
  7.2 0.1 copy.35
  7.3 0.6 pad.4.refs_6_
  7.9 0.5 compare_select_fusion.refs_8_
  8.4 229.4 %shard_map.305 = (bf16[2,4,256,2048]{3,2,1,0:T(8,128)(2,1)}, bf16[2,4,256,2048]{3,2,1,0:T(8,128)(2,1)}, bf16[2,4,256,2048]{3,2,1,0:T(8,128)(2,1)}, bf16[2,4,256,...) custom-call(bf16[256,2048]{1,0:T(8,128)(2,1)} %refs_0_.7, ...), custom_call_target="tpu_custom_call" | custom-call | tf_op jit(solution)/shard_map/pallas_call | solution.py:714
  237.9 22.1 %shard_map.306 = (bf16[2,4,256,256]{3,2,1,0:T(8,128)(2,1)}, f32[4,8,512]{2,1,0:T(8,128)}) custom-call(s32[4]{0:T(128)} %refs_0_.6, bf16[2,4,256,256]{3,2,1,0:T(8,128)(2,1)} %get-tuple-element.68.refs_1_, bf16[2,4,256,256]{3,2,1,0:T(8,128)(2,1)} %get-tuple-element.69.refs_2_, bf16[4,2,4,256,256]{4,3,2,1,0:T(8,128)(2,1)} %get-tuple-element.70.refs_3_.refs_4_, ...), custom_call_target="tpu_custom_call" | custom-call | flops 4294967296 | bytes 12582912 | tf_op jit(solution)/shard_map/pallas_call | solution.py:1707
  260.0 25.2 %shard_map.307 = (f32[2,4,256,256]{3,2,1,0:T(8,128)}, bf16[4,2,4,256,256]{4,3,2,1,0:T(8,128)(2,1)}, bf16[4,2,4,256,256]{4,3,2,1,0:T(8,128)(2,1)}) custom-call(s32[4]{0:T(128)} %refs_0_.6, bf16[2,4,256,256]{3,2,1,0:T(8,128)(2,1)} %get-tuple-element.68.refs_1_, bf16[2,4,256,256]{3,2,1,0:T(8,128)(2,1)} %get-tuple-element.69.refs_2_, ...), custom_call_target="tpu_custom_call" | custom-call | flops 10737418240 | bytes 25165824 | tf_op jit(solution)/shard_map/pallas_call | solution.py:1799
  285.1 106.5 %shard_map.308 = (f32[256,2048]{1,0:T(8,128)}, bf16[8,256,256]{2,1,0:T(8,128)(2,1)}, bf16[8,256,256]{2,1,0:T(8,128)(2,1)}, bf16[4,128,512]{2,1,0:T(8,128)(2,1)},...) custom-call(bf16[4,8,256,256]{3,2,1,0:T(8,128)(2,1)} %bitcast.39, ...), custom_call_target="tpu_custom_call" | custom-call | tf_op jit(solution)/shard_map/pallas_call | solution.py:1265
  391.7 159.8 %shard_map.309 = (bf16[64,6144]{1,0:T(8,128)(2,1)}, bf16[64,8192]{1,0:T(8,128)(2,1)}, bf16[64,2048]{1,0:T(8,128)(2,1)}, bf16[64,8192]{1,0:T(8,128)(2,1)}, f32[25...) custom-call(bf16[4,128,512]{2,1,0:T(8,128)(2,1)} %get-tuple-element.82.refs_0_, ...), custom_call_target="tpu_custom_call" | custom-call | tf_op jit(solution)/shard_map/pallas_call | solution.py:1573
  551.5 0.0 copy-start.5
  551.6 20.1 %shard_map.310 = (f32[64,6144]{1,0:T(8,128)}, f32[64,8192]{1,0:T(8,128)}, f32[64,2048]{1,0:T(8,128)}, f32[64,8192]{1,0:T(8,128)}, f32[64,6144]{1,0:T(8,128)}, /*...) custom-call(bf16[256,2048]{1,0:T(8,128)(2,1)} %refs_0_.7, ...), custom_call_target="tpu_custom_call" | custom-call | tf_op jit(solution)/shard_map/pallas_call | solution.py:1880
  571.7 0.7 multiply_subtract_fusion
  (13 shorter events, 0.1 us)
Async XLA Ops:
  2.7 1.6 copy-start
  3.2 2.1 copy-start.1
  5.3 1.1 copy-start.2
  5.3 1.8 copy-start.4
  551.5 20.1 %copy-start.3 = (f32[8,16,128]{2,1,0:T(8,128)S(1)}, f32[8,16,128]{2,1,0:T(8,128)}, u32[]{:S(2)}) copy-start(f32[8,16,128]{2,1,0:T(8,128)} %get-tuple-element.110) | copy-start | bytes 196612
  551.5 20.2 %copy-start.5 = (f32[64,13]{0,1:T(8,128)S(1)}, f32[64,13]{0,1:T(8,128)}, u32[]{:S(2)}) copy-start(f32[64,13]{0,1:T(8,128)} %param.30) | copy-start | bytes 9988
  551.6 20.2 %copy-start.6 = (f32[64,13]{0,1:T(8,128)S(1)}, f32[64,13]{0,1:T(8,128)}, u32[]{:S(2)}) copy-start(f32[64,13]{0,1:T(8,128)} %param.35) | copy-start | bytes 9988

commit v2 on v1

--- a/solution.py
+++ b/solution.py
@@ -2,6 +2,7 @@
 
 import jax
 import jax.numpy as jnp
+import numpy as np
 from jax import lax
 from jax.experimental import pallas as pl
 from jax.experimental.pallas import tpu as pltpu
@@ -391,7 +392,7 @@
     for part in to_r[0]:
         part.begin()
     start(to_t[1])
-    x_t.start(2, 1)
+    x_t.start(2)
     small_r.advance()
     for part in to_r[0]:
         part.advance()
@@ -409,10 +410,9 @@
 
     lax.fori_loop(0, 8, tables, 0)
     wait(to_t[1])
+    x_t.start(1)
     for part in to_r[1]:
         part.begin()
-    start(to_t[3])
-    start(to_t[2])
     small_r.end()
 
     smt[...] = sm[...].reshape(D, 128).T[:SMALLR, :]
@@ -556,6 +556,8 @@
                     lambda: [p.advance() for p in to_r[1]],
                     lambda: x_t.wait(2),
                     lambda: x_t.start(6),
+                    lambda: start(to_t[3]),
+                    lambda: start(to_t[2]),
                     lambda: x_t.wait(6),
                 ],
                 2: [
@@ -1498,7 +1500,6 @@
         copy.wait()
     for part in parts[1]:
         part.advance()
-    total.turn_own()
     small.both().wait_recv()
     sslots[0] = sslots[0] + blocks[place.rr_of(2)]
     small.second().start()
@@ -1520,6 +1521,7 @@
         part.gather()
         part.end()
     send_finals(2)
+    total.turn_own()
     total.end()
     for which in range(5):
         wait_finals(which)
@@ -1831,8 +1833,8 @@
 def adam_step(parameter, gradient, first_moment, second_moment, step_rate):
     first_new = BETA_ONE * first_moment + (1.0 - BETA_ONE) * gradient
     second_new = BETA_TWO * second_moment + (1.0 - BETA_TWO) * gradient * gradient
-    first_hat = first_new / (1.0 - BETA_ONE**STEPS)
-    second_hat = second_new / (1.0 - BETA_TWO**STEPS)
+    first_hat = first_new * (1.0 / (1.0 - BETA_ONE**STEPS))
+    second_hat = second_new * (1.0 / (1.0 - BETA_TWO**STEPS))
     parameter_new = parameter - step_rate * (
         first_hat / (jnp.sqrt(second_hat) + ADAM_EPS) + WEIGHT_DECAY * parameter
     )
@@ -1975,10 +1977,9 @@
     R = place.R
     rb = D // n
     turned = HEAD // 8
-    lanes = jnp.arange(HEAD // 2, dtype=jnp.int32)
-    frequency = jnp.where(
-        lanes < turned, ROPE_BASE ** (-2.0 * lanes.astype(F32) / (2 * turned)), 0.0
-    )[None, :]
+    lanes = np.arange(HEAD // 2)
+    frequency = np.where(lanes < turned, ROPE_BASE ** (-2.0 * lanes / (2 * turned)), 0.0)
+    frequency = jnp.asarray(frequency.astype(np.float32)[None, :])
 
     small_rows = jnp.pad(small_params, ((0, 0), (0, 128 - SMALLC)))
     low_in = attend_in.astype(BF)

time: 572 us -> 580 us (1.014)
  Pallas kernels: 563 us -> 573 us
where the time goes in v2:
time: 580 us; the launch traced here: 582 us
  Pallas kernels  573 us (99%)
  other arithmetic  6.36 us (1%)
    pallas_call x1, Pallas kernels, forward(): pl.pallas_call(kernel, out_shape=outs, in_specs=[ANY] * 7 + [pl.BlockSpec...  231 us
    pallas_call x1, Pallas kernels, return_two(): pl.pallas_call(kernel, out_shape=outs, in_specs=[ANY] * 14 + [VM] * 3, ou...  165 us
    pallas_call x1, Pallas kernels, return_one(): pl.pallas_call(kernel, out_shape=outs, in_specs=[ANY] * 9, out_specs=[VM]...  106 us
    pallas_call x1, Pallas kernels, attend_back(): pl.pallas_call(kernel, out_shape=[jax.ShapeDtypeStruct((2, 4, TOK, HEAD),...  26.8 us
    pallas_call x1, Pallas kernels, attend(): pl.pallas_call(kernel, out_shape=[jax.ShapeDtypeStruct((2, 4, TOK, HEAD),...  24.2 us
    pallas_call x1, Pallas kernels, adam(): pl.pallas_call(kernel, out_shape=[*outs, *own_outs], grid=(steps,), in_sp...  20.1 us

profile of v2, /device:TPU:0, one launch (start us, length us, event | category | flops | bytes accessed | tf_op | source)
XLA Modules:
  0.0 581.9 jit_solution(16128473518439304898)
XLA Ops:
  0.7 1.5 convert_element_type.14
  2.2 0.1 copy.37
  2.3 0.1 fusion.2
  2.4 0.2 fusion.3
  2.7 0.0 copy-start
  2.7 0.3 pad_maximum_fusion.1
  3.0 0.2 copy.38
  3.2 0.0 copy-start.1
  3.3 0.9 pad_maximum_fusion.refs_2_
  4.2 0.1 copy-done
  4.3 1.1 convert_element_type.15.refs_3_
  5.3 1.1 convert_element_type.17.refs_5_
  6.4 0.0 copy-done.2
  6.4 0.7 convert_element_type.16.refs_4_
  7.2 0.1 copy.36
  7.3 0.6 pad.4.refs_6_
  7.9 231.0 %shard_map.314 = (bf16[2,4,256,2048]{3,2,1,0:T(8,128)(2,1)}, bf16[2,4,256,2048]{3,2,1,0:T(8,128)(2,1)}, bf16[2,4,256,2048]{3,2,1,0:T(8,128)(2,1)}, bf16[2,4,256,...) custom-call(bf16[256,2048]{1,0:T(8,128)(2,1)} %refs_0_.7, ...), custom_call_target="tpu_custom_call" | custom-call | tf_op jit(solution)/shard_map/pallas_call | solution.py:716
  238.9 24.2 %shard_map.315 = (bf16[2,4,256,256]{3,2,1,0:T(8,128)(2,1)}, f32[4,8,512]{2,1,0:T(8,128)}) custom-call(s32[4]{0:T(128)} %refs_0_.6, bf16[2,4,256,256]{3,2,1,0:T(8,128)(2,1)} %get-tuple-element.68.refs_1_, bf16[2,4,256,256]{3,2,1,0:T(8,128)(2,1)} %get-tuple-element.69.refs_2_, bf16[4,2,4,256,256]{4,3,2,1,0:T(8,128)(2,1)} %get-tuple-element.70.refs_3_.refs_4_, ...), custom_call_target="tpu_custom_call" | custom-call | flops 4294967296 | bytes 12582912 | tf_op jit(solution)/shard_map/pallas_call | solution.py:1709
  263.1 26.8 %shard_map.316 = (f32[2,4,256,256]{3,2,1,0:T(8,128)}, bf16[4,2,4,256,256]{4,3,2,1,0:T(8,128)(2,1)}, bf16[4,2,4,256,256]{4,3,2,1,0:T(8,128)(2,1)}) custom-call(s32[4]{0:T(128)} %refs_0_.6, bf16[2,4,256,256]{3,2,1,0:T(8,128)(2,1)} %get-tuple-element.68.refs_1_, bf16[2,4,256,256]{3,2,1,0:T(8,128)(2,1)} %get-tuple-element.69.refs_2_, ...), custom_call_target="tpu_custom_call" | custom-call | flops 10737418240 | bytes 25165824 | tf_op jit(solution)/shard_map/pallas_call | solution.py:1801
  289.9 105.9 %shard_map.317 = (f32[256,2048]{1,0:T(8,128)}, bf16[8,256,256]{2,1,0:T(8,128)(2,1)}, bf16[8,256,256]{2,1,0:T(8,128)(2,1)}, bf16[4,128,512]{2,1,0:T(8,128)(2,1)},...) custom-call(bf16[4,8,256,256]{3,2,1,0:T(8,128)(2,1)} %bitcast.39, ...), custom_call_target="tpu_custom_call" | custom-call | tf_op jit(solution)/shard_map/pallas_call | solution.py:1267
  395.8 165.2 %shard_map.318 = (bf16[64,6144]{1,0:T(8,128)(2,1)}, bf16[64,8192]{1,0:T(8,128)(2,1)}, bf16[64,2048]{1,0:T(8,128)(2,1)}, bf16[64,8192]{1,0:T(8,128)(2,1)}, f32[25...) custom-call(bf16[4,128,512]{2,1,0:T(8,128)(2,1)} %get-tuple-element.82.refs_0_, ...), custom_call_target="tpu_custom_call" | custom-call | tf_op jit(solution)/shard_map/pallas_call | solution.py:1575
  561.1 0.0 copy-start.6
  561.1 20.1 %shard_map.319 = (f32[64,6144]{1,0:T(8,128)}, f32[64,8192]{1,0:T(8,128)}, f32[64,2048]{1,0:T(8,128)}, f32[64,8192]{1,0:T(8,128)}, f32[64,6144]{1,0:T(8,128)}, /*...) custom-call(bf16[256,2048]{1,0:T(8,128)(2,1)} %refs_0_.7, ...), custom_call_target="tpu_custom_call" | custom-call | tf_op jit(solution)/shard_map/pallas_call | solution.py:1882
  581.2 0.7 multiply_subtract_fusion
  (12 shorter events, 0.1 us)
Async XLA Ops:
  2.7 1.6 copy-start
  3.2 2.1 copy-start.1
  5.3 1.1 copy-start.2
  5.3 1.8 copy-start.4
  561.0 20.1 %copy-start.3 = (f32[8,16,128]{2,1,0:T(8,128)S(1)}, f32[8,16,128]{2,1,0:T(8,128)}, u32[]{:S(2)}) copy-start(f32[8,16,128]{2,1,0:T(8,128)} %get-tuple-element.110) | copy-start | bytes 196612
  561.1 20.2 %copy-start.5 = (f32[64,13]{0,1:T(8,128)S(1)}, f32[64,13]{0,1:T(8,128)}, u32[]{:S(2)}) copy-start(f32[64,13]{0,1:T(8,128)} %param.31) | copy-start | bytes 9988
  561.1 20.2 %copy-start.6 = (f32[64,13]{0,1:T(8,128)S(1)}, f32[64,13]{0,1:T(8,128)}, u32[]{:S(2)}) copy-start(f32[64,13]{0,1:T(8,128)} %param.36) | copy-start | bytes 9988

commit v3 on v2

--- a/solution.py
+++ b/solution.py
@@ -223,17 +223,31 @@
         for s in range(1, 8):
             hop = top_bit(s)
             src = own if s == hop else out.at[(s - hop) // 4, (s - hop) % 4]
-            self.ops[s] = net.add(
-                lambda k, src=src, s=s, hop=hop: (src, out.at[s // 4, s % 4], place.dev_t(hop))
-            )
+            dst = out.at[s // 4, s % 4]
+            parts = [slice(None)]
+            if s in (1, 3):
+                parts = [pl.ds(h * (D // 2), D // 2) for h in range(2)]
+            for h, cols in enumerate(parts):
+                self.ops[s, h] = net.add(
+                    lambda k, src=src, dst=dst, cols=cols, hop=hop: (
+                        src.at[:, cols], dst.at[:, cols], place.dev_t(hop),
+                    )
+                )
+
+    def named(self, which):
+        if isinstance(which, tuple):
+            return [self.ops[which]]
+        return [op for (s, _), op in self.ops.items() if s == which]
 
     def start(self, *which):
         for s in which:
-            self.ops[s]().start()
+            for op in self.named(s):
+                op().start()
 
     def wait(self, *which):
         for s in which:
-            self.ops[s]().wait_recv()
+            for op in self.named(s):
+                op().wait_recv()
 
 
 class GatherR:
@@ -305,7 +319,7 @@
 def forward_kernel(
     n, nseq, x, gy, wi, wu, wo, wd, small, lengths, frequency,
     xg, gg, a1g, a2g, oi, ou, oo, od, qo, kg, vg, zo, dho, dout, smt, sums, stats, cosine, sine,
-    xv, gv, sm, ti, tu, to, td, slope, a2v, kt, vt, at, ztile, dht, bias, dhsum,
+    xv, gv, sm, ti, tu, to, td, slope, a2v, qkv, at, ztile, dht, bias, dhsum,
     send, recv, local, out_sem, g_sem,
 ):
     place = Place(n)
@@ -344,7 +358,7 @@
     g_t = GatherT(net, place, gy, gv)
     both = orders(place.bits)
     keys = []
-    for own, out, order in ((kt, kg, both[0]), (vt, vg, both[1])):
+    for own, out, order in ((qkv.at[1], kg, both[0]), (qkv.at[2], vg, both[1])):
         ops = {}
         for i, bit in spread(order):
             ops[i] = net.add(
@@ -494,10 +508,18 @@
 
     def hidden_units(k):
         u = place_of(k)
-        hidden = jnp.dot(
-            a2v[:, u].reshape(RUN, D), tu[...].reshape(D, FFT), preferred_element_type=F32
-        )
-        slope[:, u] = (hidden + bias[1:2, :]).reshape(2, TOK, FFT)
+
+        def columns_of(c, carry):
+            cols = pl.ds(pl.multiple_of(c * HEAD, HEAD), HEAD)
+            hidden = jnp.dot(
+                a2v[:, u].reshape(RUN, D),
+                tu[:, :, :, cols].reshape(D, HEAD),
+                preferred_element_type=F32,
+            )
+            slope[:, u, :, cols] = (hidden + bias[1:2, cols]).reshape(2, TOK, HEAD)
+            return carry
+
+        lax.fori_loop(0, FFT // HEAD, columns_of, 0)
         free(ztile, zo, k, 1)
 
         def chunk(r, carry):
@@ -523,24 +545,28 @@
         u = place_of(k)
         free(at, a1g, k, 0)
         norms(u)
-        joint = (
-            jnp.dot(
-                at[...].reshape(RUN, D), ti[...].reshape(D, 3 * HEAD), preferred_element_type=F32
+        half = HEAD // 2
+
+        def part(p, carry):
+            cols = pl.ds(pl.multiple_of(p * HEAD, HEAD), HEAD)
+            joint = jnp.dot(
+                at[...].reshape(RUN, D),
+                ti[:, :, :, cols].reshape(D, HEAD),
+                preferred_element_type=F32,
             )
-            + bias[0:1, : 3 * HEAD]
-        )
+            joint += bias[0:1, cols]
+            turned = p < 2
+            cs = jnp.where(turned, cosine[:, u].reshape(RUN, half), 1.0)
+            sn = jnp.where(turned, sine[:, u].reshape(RUN, half), 0.0)
+            scale = jnp.where(p == 0, HEAD**-0.5, 1.0).astype(F32)
+            one, two = joint[:, :half], joint[:, half:]
+            for at_col, value in ((0, one * cs - two * sn), (half, two * cs + one * sn)):
+                value = (value.astype(BF).astype(F32) * scale).astype(BF)
+                qkv[p, :, u, :, at_col : at_col + half] = value.reshape(2, TOK, half)
+            return carry
+
+        lax.fori_loop(0, 3, part, 0)
         staged(at, a1g, u, 0).start()
-        half = HEAD // 2
-        cs, sn = cosine[:, u].reshape(RUN, half), sine[:, u].reshape(RUN, half)
-        for p, (dst, scale) in enumerate(((qo, HEAD**-0.5), (kt, None))):
-            one = joint[:, p * HEAD : p * HEAD + half]
-            two = joint[:, p * HEAD + half : (p + 1) * HEAD]
-            for at_col, value in ((0, one * cs - two * sn), (half, two * cs + one * sn)):
-                value = value.astype(BF)
-                if scale is not None:
-                    value = (value.astype(F32) * scale).astype(BF)
-                dst[:, u, :, at_col : at_col + half] = value.reshape(2, TOK, half)
-        vt[:, u] = joint[:, 2 * HEAD :].astype(BF).reshape(2, TOK, HEAD)
         for core in range(2):
             for ops, plan in keys:
                 for i, bit in plan:
@@ -561,8 +587,10 @@
                     lambda: x_t.wait(6),
                 ],
                 2: [
-                    lambda: x_t.wait(1),
-                    lambda: x_t.start(3, 5),
+                    lambda: x_t.wait((1, 0)),
+                    lambda: x_t.start((3, 0)),
+                    lambda: x_t.wait((1, 1)),
+                    lambda: x_t.start((3, 1), 5),
                     lambda: [p.end() for p in to_r[1]],
                     lambda: pltpu.make_async_copy(tu, ou, local.at[1]).start(),
                 ],
@@ -580,7 +608,8 @@
                     lambda: g_t.start(2),
                     lambda: x_t.wait(7),
                 ],
-                7: [lambda: g_t.wait(1), lambda: g_t.start(3, 5)],
+                6: [lambda: g_t.wait((1, 0)), lambda: g_t.start((3, 0))],
+                7: [lambda: g_t.wait((1, 1)), lambda: g_t.start((3, 1), 5)],
             },
         )
         late = k // 4
@@ -603,8 +632,9 @@
 
     lax.fori_loop(0, 8, first, 0)
     own_out = [
-        pltpu.make_async_copy(kt, kg.at[0], local.at[4]),
-        pltpu.make_async_copy(vt, vg.at[0], local.at[5]),
+        pltpu.make_async_copy(qkv.at[1], kg.at[0], local.at[4]),
+        pltpu.make_async_copy(qkv.at[2], vg.at[0], local.at[5]),
+        pltpu.make_async_copy(qkv.at[0], qo, local.at[7]),
         pltpu.make_async_copy(xv, xg, local.at[6]),
         pltpu.make_async_copy(a2v, a2g, local.at[8]),
     ]
@@ -643,12 +673,21 @@
         )
         free(dht, dho, k, 2)
         pltpu.make_async_copy(gv.at[:, u], gg.at[:, u], g_sem.at[u]).start()
+        def columns_of(c, carry):
+            cols = pl.ds(pl.multiple_of(c * HEAD, HEAD), HEAD)
+            dz = jnp.dot(
+                gv[:, u].reshape(RUN, D),
+                td[:, :, :, cols].reshape(D, HEAD),
+                preferred_element_type=F32,
+            )
+            dh = (dz * slope[:, u, :, cols].reshape(RUN, HEAD)).astype(BF)
+            dht[:, :, cols] = dh.reshape(2, TOK, HEAD)
+            dhsum[0:1, cols] += jnp.sum(dh.astype(F32), axis=0, keepdims=True)
+            return carry
+
+        lax.fori_loop(0, FFT // HEAD, columns_of, 0)
+        staged(dht, dho, u, 2).start()
         grad = gv[:, u].reshape(RUN, D)
-        dz = jnp.dot(grad, td[...].reshape(D, FFT), preferred_element_type=F32)
-        dh = (dz * slope[:, u].reshape(RUN, FFT)).astype(BF)
-        dht[...] = dh.reshape(2, TOK, FFT)
-        staged(dht, dho, u, 2).start()
-        dhsum[0:1, :] += jnp.sum(dh.astype(F32), axis=0, keepdims=True)
         dout[:, u] = (
             jnp.dot(grad, to[...].reshape(D, HEAD), preferred_element_type=F32)
             .astype(BF)
@@ -692,7 +731,7 @@
     outs += [shape(*head), shape(SMALLR, D, kind=F32), shape(SMALLR, D, kind=F32)]
     outs += [shape(2, 4, TOK, 128, kind=F32)]
     outs += [shape(2, 4, TOK, HEAD // 2, kind=F32) for _ in range(2)]
-    out_specs = [ANY] * 8 + [VM] + [ANY] * 4 + [VM] * 6
+    out_specs = [ANY] * 13 + [VM] * 6
     scratch = [
         pltpu.VMEM(block, BF),
         pltpu.VMEM(block, BF),
@@ -700,15 +739,14 @@
         *[pltpu.VMEM(w, BF) for w in w_shapes],
         pltpu.VMEM(cols, F32),
         pltpu.VMEM(block, BF),
-        pltpu.VMEM(head, BF),
-        pltpu.VMEM(head, BF),
+        pltpu.VMEM((3, *head), BF),
         pltpu.VMEM((2, TOK, D), BF),
         pltpu.VMEM((2, TOK, FFT), BF),
         pltpu.VMEM((2, TOK, FFT), BF),
         pltpu.VMEM((8, FFT), F32),
         pltpu.VMEM((8, FFT), F32),
     ]
-    copies = 7 + 7 * 6 + (R - 1) * (1 + 8 + 2 * 8) + 14
+    copies = 7 + 7 * 6 + (R - 1) * (1 + 8 + 2 * 8) + 18
 
     def kernel(*refs):
         forward_kernel(n, lengths.shape[0], *refs)
@@ -990,12 +1028,21 @@
     def __init__(self, net, place, data, cs, zs, ys, out):
         self.data, self.cs, self.zs, self.ys, self.out = data, cs, zs, ys, out
         self.hop_c = net.add(lambda k: (data.at[k], cs.at[k], place.dev_t(4)), 4)
-        self.hop_z0 = net.add(lambda k: (cs.at[2 + k], zs.at[k], place.dev_t(2)), 2)
-        self.hop_z1 = net.add(lambda k: (zs.at[1], ys.at[0], place.dev_t(1)))
+        self.near_z0 = net.add(lambda k: (cs.at[2], zs.at[0], place.dev_t(2)))
+        halves = [(slice(None), pl.ds(h * (D // 2), D // 2)) for h in range(2)]
+        self.halves = halves
+        self.far_z0 = [
+            net.add(lambda k, h=h: (cs.at[(3, *h)], zs.at[(1, *h)], place.dev_t(2)))
+            for h in halves
+        ]
+        self.hop_z1 = [
+            net.add(lambda k, h=h: (zs.at[(1, *h)], ys.at[(0, *h)], place.dev_t(1)))
+            for h in halves
+        ]
 
     @staticmethod
     def order(idx):
-        return 7 - idx // 4 - 2 * (idx % 4)
+        return 7 - 4 * (idx % 2) - 2 * (idx // 2 % 2) - idx // 4
 
     def loop(self, make, emit, after):
         def step(idx, carry):
@@ -1019,27 +1066,37 @@
                 self.hop_c(k).wait_recv()
                 emit(s, idx, near)
 
-                @pl.when(s >= 2)
+                @pl.when(s == 3)
                 def _():
-                    self.hop_z0(s - 2).start()
+                    self.far_z0[0]().start()
+
+                @pl.when(s == 2)
+                def _():
+                    self.near_z0().start()
 
             after(idx)
             return carry
 
         lax.fori_loop(0, 8, step, 0)
 
-    def turn_z1(self):
-        self.hop_z0(1).wait_recv()
-        add_rows(self.zs.at[1], self.cs.at[1], self.zs.at[1])
-        self.hop_z1().start()
+    def more(self):
+        self.far_z0[1]().start()
+
+    def turn(self, h):
+        self.far_z0[h]().wait_recv()
+        mine, there = self.cs.at[(1, *self.halves[h])], self.zs.at[(1, *self.halves[h])]
+        add_rows(there, mine, there)
+        self.hop_z1[h]().start()
 
     def turn_own(self):
-        self.hop_z0(0).wait_recv()
+        self.near_z0().wait_recv()
         add_rows(self.zs.at[0], self.cs.at[0], self.zs.at[0])
 
     def end(self):
-        self.hop_z1().wait_recv()
-        add_rows(self.out, self.zs.at[0], self.ys.at[0])
+        for h in range(2):
+            self.hop_z1[h]().wait_recv()
+            where = self.halves[h]
+            add_rows(self.out.at[where], self.zs.at[(0, *where)], self.ys.at[(0, *where)])
 
 
 def fold_scratch():
@@ -1093,7 +1150,7 @@
     return halves, pieces
 
 
-def gradient_tiles(lhs, tiles, sem, products):
+def gradient_tiles(lhs, tiles, turned, sem, products):
     wide = tiles.shape[-1]
     count = D // wide
 
@@ -1114,15 +1171,25 @@
         def _():
             fetch(f + 1).start()
 
-        left = tiles[f % 2].reshape(8 * TOK, wide)
+        def turn_block(s, carry):
+            turned[:, pl.ds(pl.multiple_of(s * TOK, TOK), TOK)] = tiles[f % 2, s].T
+            return carry
+
+        lax.fori_loop(0, 8, turn_block, 0)
         for rhs, stage, out, sems in products:
 
             @pl.when(f >= 2)
             def _(stage=stage, out=out, sems=sems):
                 put(f - 2, stage, out, sems).wait()
 
-            right = rhs[...].reshape(8 * TOK, rhs.shape[-1])
-            stage[f % 2] = contract_rows(left, right).astype(BF)
+            def columns_of(c, carry, rhs=rhs, stage=stage):
+                cols = pl.ds(pl.multiple_of(c * HEAD, HEAD), HEAD)
+                right = rhs[:, :, cols].reshape(8 * TOK, HEAD)
+                total = jnp.dot(turned[...], right, preferred_element_type=F32)
+                stage[f % 2, :, cols] = total.astype(BF)
+                return carry
+
+            lax.fori_loop(0, rhs.shape[-1] // HEAD, columns_of, 0)
             put(f, stage, out, sems).start()
         return carry
 
@@ -1146,7 +1213,7 @@
 def return_one_kernel(
     n, dk, dv, o, z, w_out, w_down, gy, a2, dh,
     p_own, dk_own, dv_own, up_sum, g_out, g_down, g_up,
-    zov, wdo, dhv, kown, vown, data, cs, zs, ys, ks, vs, tiles, st_wide, st_head, uown, us,
+    zov, wdo, dhv, kown, vown, data, cs, zs, ys, ks, vs, tiles, turned, st_wide, st_head, uown, us,
     send, recv, load, fetch_sem, put_sem, near,
 ):
     place = Place(n)
@@ -1187,24 +1254,37 @@
         del s, idx
 
     def emit(s, idx, put):
-        put((slice(None), slice(None)), contract_cols(zov[s], wdo[...]))
+        def chunk(k, carry):
+            cols = pl.ds(pl.multiple_of(k * HEAD, HEAD), HEAD)
+            put((slice(None), cols), contract_cols(zov[s], wdo[cols, :]))
+            return carry
+
+        lax.fori_loop(0, D // HEAD, chunk, 0)
 
     def after(idx):
         @pl.when(idx == 3)
         def _():
+            total.more()
             keys.first().start()
             values.first().start()
 
-        @pl.when(idx == 6)
+        @pl.when(idx == 4)
+        def _():
+            total.turn(0)
+
+        @pl.when(idx == 5)
         def _():
             for copy in loads[4:]:
                 copy.wait()
             keys.advance()
             values.advance()
 
+        @pl.when(idx == 6)
+        def _():
+            total.turn(1)
+
     total.loop(make, emit, after)
-    total.turn_z1()
-    gradient_tiles(a2, tiles, fetch_sem, [(dhv, st_wide, g_up, put_sem.at[0])])
+    gradient_tiles(a2, tiles, turned, fetch_sem, [(dhv, st_wide, g_up, put_sem.at[0])])
     own_loads = [
         pltpu.make_async_copy(src, dst, near.at[k]) for k, (src, dst) in enumerate(pieces)
     ]
@@ -1214,7 +1294,7 @@
     keys.gather()
     values.gather()
     gradient_tiles(
-        gy, tiles, fetch_sem,
+        gy, tiles, turned, fetch_sem,
         [
             (zov.at[:, :, :FFT], st_wide, g_down, put_sem.at[0]),
             (zov.at[:, :, FFT:], st_head, g_out, put_sem.at[1]),
@@ -1255,6 +1335,7 @@
         pltpu.VMEM((3, *head), BF),
         pltpu.VMEM((3, *head), BF),
         pltpu.VMEM((2, 8, TOK, WIDE), BF),
+        pltpu.VMEM((WIDE, 8 * TOK), BF),
         pltpu.VMEM((2, WIDE, FFT), BF),
         pltpu.VMEM((2, WIDE, HEAD), BF),
         pltpu.VMEM((2, *half), BF),
@@ -1271,8 +1352,8 @@
         out_specs=[VM] * 4 + [ANY] * 3,
         scratch_shapes=[
             *scratch,
-            pltpu.SemaphoreType.DMA((16,)),
-            pltpu.SemaphoreType.DMA((16,)),
+            pltpu.SemaphoreType.DMA((18,)),
+            pltpu.SemaphoreType.DMA((18,)),
             pltpu.SemaphoreType.DMA((9,)),
             pltpu.SemaphoreType.DMA((2,)),
             pltpu.SemaphoreType.DMA((2, 2)),
@@ -1287,8 +1368,8 @@
 def return_two_kernel(
     n, gi, gu0, gu, go, gd, dq, dk, dv, a1, x, dh, w_in, w_up, cosine, sine, smt, stats, sums,
     oi, ou, oo, od, e_own, osmall, gi_out,
-    dqv, dkv, dvv, djp, djn, dhv, wi, wu, xt, cst, snt, data, cs, zs, ys, tile, other,
-    uown, us, ui, uo, ud, si, so, sd, term, blocks, sslots, tiles, st_in,
+    dqv, dkv, dvv, djp, djn, dhv, wi, wu, xt, cst, snt, data, cs, zs, ys,
+    uown, us, ui, uo, ud, si, so, sd, term, blocks, sslots, tiles, turned, st_in,
     send, recv, load, near, x_sem, fetch_sem, put_sem, last_sem,
 ):
     del gi
@@ -1375,6 +1456,8 @@
                 op().wait_recv()
 
     up.begin()
+    for part in parts[0]:
+        part.begin()
     send_finals(3)
     loads = [
         pltpu.make_async_copy(src, dst, load.at[k])
@@ -1405,34 +1488,42 @@
         copy.wait()
     chunk_cols = 256
 
-    def joint(s):
+    def paired_joint(s):
         csn, sn = cst[s], snt[s]
         half = HEAD // 2
         for p, src in enumerate((dqv, dkv)):
             one = src[s, :, :half].astype(F32)
             two = src[s, :, half:].astype(F32)
-            cols = slice(p * HEAD, (p + 1) * HEAD)
             djp[:, p * HEAD : p * HEAD + half] = (one * csn + two * sn).astype(BF)
             djp[:, p * HEAD + half : (p + 1) * HEAD] = (two * csn - one * sn).astype(BF)
+        djp[:, 2 * HEAD :] = dvv[s]
+
+    def natural_joint(s):
+        for p in range(2):
+            cols = slice(p * HEAD, (p + 1) * HEAD)
             natural = contract_cols(djp[:, cols], shuffle)
             djn[s, :, cols] = natural.astype(BF)
             term[4 + p : 5 + p, head_cols] += jnp.sum(natural, axis=0, keepdims=True)
         value = dvv[s]
-        djp[:, 2 * HEAD :] = value
         djn[s, :, 2 * HEAD :] = value
         term[6:7, head_cols] += jnp.sum(value.astype(F32), axis=0, keepdims=True)
 
     def make(s, idx):
-        joint(s)
+        @pl.when(idx < 4)
+        def _():
+            paired_joint(s)
+            natural_joint(s)
+
+        @pl.when(idx >= 4)
+        def _():
+            paired_joint(s)
+
         fetch_x(s, idx % 2).wait()
 
         @pl.when(idx < 7)
         def _():
             fetch_x(total.order(idx + 1), (idx + 1) % 2).start()
 
-        tile[...] = contract_cols(djp[...], wi[...])
-        other[...] = contract_cols(dhv[s], wu[...])
-
     def emit(s, idx, put):
         average = stats[s, :, 0:1]
         inverse = stats[s, :, 1:2]
@@ -1440,7 +1531,8 @@
         def chunk(k, carry):
             cols = pl.ds(pl.multiple_of(k * chunk_cols, chunk_cols), chunk_cols)
             xhat = (xt[idx % 2, :, cols].astype(F32) - average) * inverse
-            one, two = tile[:, cols], other[:, cols]
+            one = contract_cols(djp[...], wi[cols, :])
+            two = contract_cols(dhv[s], wu[cols, :])
             for row, value in ((0, one * xhat), (1, one), (2, two * xhat), (3, two)):
                 term[row : row + 1, cols] += jnp.sum(value, axis=0, keepdims=True)
             put((slice(None), cols), one * smt[0:1, cols] + two * smt[2:3, cols])
@@ -1451,33 +1543,60 @@
     def after(idx):
         @pl.when(idx == 1)
         def _():
-            for part in parts[0]:
-                part.begin()
-
-        @pl.when(idx == 3)
-        def _():
             for copy in own_loads[12:]:
                 copy.wait()
             up.advance()
+
+        @pl.when(idx == 2)
+        def _():
+            total.more()
+            for copy in own_loads[:4]:
+                copy.wait()
+            for part in parts[0]:
+                part.advance()
+            up.gather()
+            up.end()
+            send_finals(4)
+
+        @pl.when(idx == 3)
+        def _():
+            total.turn(0)
+
+            def rest(k, carry):
+                paired_joint(6 - 2 * k)
+                natural_joint(6 - 2 * k)
+                return carry
+
+            lax.fori_loop(0, 4, rest, 0)
+            gradient_tiles(a1, tiles, turned, fetch_sem, [(djn, st_in, gi_out, put_sem)])
+            for part in parts[2]:
+                part.begin()
+            for copy in own_loads[8:12]:
+                copy.start()
+            total.turn(1)
+            for part in parts[0]:
+                part.gather()
+                part.end()
+            send_finals(0)
 
         @pl.when(idx == 4)
         def _():
             for part in parts[1]:
                 part.begin()
 
-        @pl.when(idx == 5)
-        def _():
-            up.gather()
-            up.end()
-            send_finals(4)
-
         @pl.when(idx == 6)
         def _():
-            for copy in own_loads[:4]:
+            for copy in own_loads[8:12]:
                 copy.wait()
-            for part in parts[0]:
+            for part in parts[2]:
                 part.advance()
-            total.turn_z1()
+
+        @pl.when(idx == 7)
+        def _():
+            for copy in own_loads[4:8]:
+                copy.wait()
+            for part in parts[1]:
+                part.advance()
 
     total.loop(make, emit, after)
 
@@ -1487,41 +1606,24 @@
             blocks[rr, zt] = term[:, at : at + 128]
     small.both().start()
     small.first().start()
-    gradient_tiles(a1, tiles, fetch_sem, [(djn, st_in, gi_out, put_sem)])
     for part in parts[2]:
-        part.begin()
-    for copy in own_loads[8:12]:
-        copy.start()
-    for part in parts[0]:
         part.gather()
         part.end()
-    send_finals(0)
-    for copy in own_loads[4:8]:
-        copy.wait()
-    for part in parts[1]:
-        part.advance()
-    small.both().wait_recv()
-    sslots[0] = sslots[0] + blocks[place.rr_of(2)]
-    small.second().start()
-    for copy in own_loads[8:12]:
-        copy.wait()
-    for part in parts[2]:
-        part.advance()
+    send_finals(2)
     for part in parts[1]:
         part.gather()
         part.end()
     send_finals(1)
+    small.both().wait_recv()
+    sslots[0] = sslots[0] + blocks[place.rr_of(2)]
+    small.second().start()
+    total.turn_own()
     small.first().wait_recv()
     small.second().wait_recv()
     sslots[2] = sslots[2] + (sslots[1] + blocks[place.rr])
     small_mine.start()
     for op in small_last:
         op().start()
-    for part in parts[2]:
-        part.gather()
-        part.end()
-    send_finals(2)
-    total.turn_own()
     total.end()
     for which in range(5):
         wait_finals(which)
@@ -1555,8 +1657,6 @@
         pltpu.VMEM((8, TOK, HEAD // 2), F32),
         pltpu.VMEM((8, TOK, HEAD // 2), F32),
         *fold_scratch(),
-        pltpu.VMEM((TOK, D), F32),
-        pltpu.VMEM((TOK, D), F32),
         pltpu.VMEM((2, 4, 2 * rb, FFT // 2), BF),
         pltpu.VMEM((3, 4, 2 * rb, FFT // 2), BF),
         *[pltpu.VMEM((2, 2, 2, 2 * rb, wide[k]), BF) for k in (0, 2, 3)],
@@ -1565,9 +1665,10 @@
         pltpu.VMEM((R, 4, SMALLR, 128), F32),
         pltpu.VMEM((3, 4, SMALLR, 128), F32),
         pltpu.VMEM((2, 8, TOK, HEAD), BF),
+        pltpu.VMEM((HEAD, 8 * TOK), BF),
         pltpu.VMEM((2, HEAD, 3 * HEAD), BF),
     ]
-    copies = 6 * 3 + 3 + 3 + 7 + 7 * 7 + 7
+    copies = 6 * 3 + 3 + 3 + 9 + 7 * 7 + 7
 
     def kernel(*refs):
         return_two_kernel(n, None, *refs)

time: 580 us -> 579 us (level)
    pallas_call x1, Pallas kernels: 106 us -> 116 us  [return_one(): pl.pallas_call(kernel, out_shape=outs, in_specs=[ANY] * 9, out_specs=[VM]...]
    pallas_call x1, Pallas kernels: 165 us -> 157 us  [return_two(): pl.pallas_call(kernel, out_shape=outs, in_specs=[ANY] * 14 + [VM] * 3, ou...]
    pallas_call x1, Pallas kernels: 24.2 us -> 17.9 us  [attend(): pl.pallas_call(kernel, out_shape=[jax.ShapeDtypeStruct((2, 4, TOK, HEAD),...]
where the time goes in v3:
time: 579 us; the launch traced here: 576 us
  Pallas kernels  568 us (98%)
  other arithmetic  6.36 us (1%)
    pallas_call x1, Pallas kernels, forward(): pl.pallas_call(kernel, out_shape=outs, in_specs=[ANY] * 7 + [pl.BlockSpec...  234 us
    pallas_call x1, Pallas kernels, return_two(): pl.pallas_call(kernel, out_shape=outs, in_specs=[ANY] * 14 + [VM] * 3, ou...  157 us
    pallas_call x1, Pallas kernels, return_one(): pl.pallas_call(kernel, out_shape=outs, in_specs=[ANY] * 9, out_specs=[VM]...  116 us
    pallas_call x1, Pallas kernels, attend_back(): pl.pallas_call(kernel, out_shape=[jax.ShapeDtypeStruct((2, 4, TOK, HEAD),...  22.6 us
    pallas_call x1, Pallas kernels, adam(): pl.pallas_call(kernel, out_shape=[*outs, *own_outs], grid=(steps,), in_sp...  20.1 us
    pallas_call x1, Pallas kernels, attend(): pl.pallas_call(kernel, out_shape=[jax.ShapeDtypeStruct((2, 4, TOK, HEAD),...  17.9 us

profile of v3, /device:TPU:0, one launch (start us, length us, event | category | flops | bytes accessed | tf_op | source)
XLA Modules:
  0.0 576.4 jit_solution(15775062271067707813)
XLA Ops:
  0.7 1.5 convert_element_type.14
  2.2 0.1 copy.37
  2.3 0.1 fusion.2
  2.4 0.2 fusion.3
  2.7 0.0 copy-start
  2.7 0.3 pad_maximum_fusion.1
  3.0 0.2 copy.38
  3.2 0.0 copy-start.1
  3.3 0.9 pad_maximum_fusion.refs_2_
  4.2 0.1 copy-done
  4.3 1.1 convert_element_type.15.refs_3_
  5.3 1.1 convert_element_type.17.refs_5_
  6.4 0.0 copy-done.2
  6.4 0.7 convert_element_type.16.refs_4_
  7.2 0.1 copy.36
  7.3 0.6 pad.4.refs_6_
  7.9 233.8 %shard_map.314 = (bf16[2,4,256,2048]{3,2,1,0:T(8,128)(2,1)}, bf16[2,4,256,2048]{3,2,1,0:T(8,128)(2,1)}, bf16[2,4,256,2048]{3,2,1,0:T(8,128)(2,1)}, bf16[2,4,256,...) custom-call(bf16[256,2048]{1,0:T(8,128)(2,1)} %refs_0_.7, ...), custom_call_target="tpu_custom_call" | custom-call | tf_op jit(solution)/shard_map/pallas_call | solution.py:754
  241.7 17.9 %shard_map.315 = (bf16[2,4,256,256]{3,2,1,0:T(8,128)(2,1)}, f32[4,8,512]{2,1,0:T(8,128)}) custom-call(s32[4]{0:T(128)} %refs_0_.6, bf16[2,4,256,256]{3,2,1,0:T(8,128)(2,1)} %get-tuple-element.68.refs_1_, bf16[2,4,256,256]{3,2,1,0:T(8,128)(2,1)} %get-tuple-element.69.refs_2_, bf16[4,2,4,256,256]{4,3,2,1,0:T(8,128)(2,1)} %get-tuple-element.70.refs_3_.refs_4_, ...), custom_call_target="tpu_custom_call" | custom-call | flops 4294967296 | bytes 12582912 | tf_op jit(solution)/shard_map/pallas_call | solution.py:1810
  259.6 22.6 %shard_map.316 = (f32[2,4,256,256]{3,2,1,0:T(8,128)}, bf16[4,2,4,256,256]{4,3,2,1,0:T(8,128)(2,1)}, bf16[4,2,4,256,256]{4,3,2,1,0:T(8,128)(2,1)}) custom-call(s32[4]{0:T(128)} %refs_0_.6, bf16[2,4,256,256]{3,2,1,0:T(8,128)(2,1)} %get-tuple-element.68.refs_1_, bf16[2,4,256,256]{3,2,1,0:T(8,128)(2,1)} %get-tuple-element.69.refs_2_, ...), custom_call_target="tpu_custom_call" | custom-call | flops 10737418240 | bytes 25165824 | tf_op jit(solution)/shard_map/pallas_call | solution.py:1902
  282.2 116.5 %shard_map.317 = (f32[256,2048]{1,0:T(8,128)}, bf16[8,256,256]{2,1,0:T(8,128)(2,1)}, bf16[8,256,256]{2,1,0:T(8,128)(2,1)}, bf16[4,128,512]{2,1,0:T(8,128)(2,1)},...) custom-call(bf16[4,8,256,256]{3,2,1,0:T(8,128)(2,1)} %bitcast.39, ...), custom_call_target="tpu_custom_call" | custom-call | tf_op jit(solution)/shard_map/pallas_call | solution.py:1348
  398.7 156.8 %shard_map.318 = (bf16[64,6144]{1,0:T(8,128)(2,1)}, bf16[64,8192]{1,0:T(8,128)(2,1)}, bf16[64,2048]{1,0:T(8,128)(2,1)}, bf16[64,8192]{1,0:T(8,128)(2,1)}, f32[25...) custom-call(bf16[4,128,512]{2,1,0:T(8,128)(2,1)} %get-tuple-element.82.refs_0_, ...), custom_call_target="tpu_custom_call" | custom-call | tf_op jit(solution)/shard_map/pallas_call | solution.py:1676
  555.5 0.0 copy-start.5
  555.6 20.1 %shard_map.319 = (f32[64,6144]{1,0:T(8,128)}, f32[64,8192]{1,0:T(8,128)}, f32[64,2048]{1,0:T(8,128)}, f32[64,8192]{1,0:T(8,128)}, f32[64,6144]{1,0:T(8,128)}, /*...) custom-call(bf16[256,2048]{1,0:T(8,128)(2,1)} %refs_0_.7, ...), custom_call_target="tpu_custom_call" | custom-call | tf_op jit(solution)/shard_map/pallas_call | solution.py:1983
  575.7 0.7 multiply_subtract_fusion
  (12 shorter events, 0.1 us)
Async XLA Ops:
  2.7 1.6 copy-start
  3.2 2.1 copy-start.1
  5.3 1.1 copy-start.2
  5.3 1.8 copy-start.4
  555.5 20.1 %copy-start.3 = (f32[8,16,128]{2,1,0:T(8,128)S(1)}, f32[8,16,128]{2,1,0:T(8,128)}, u32[]{:S(2)}) copy-start(f32[8,16,128]{2,1,0:T(8,128)} %get-tuple-element.110) | copy-start | bytes 196612
  555.5 20.2 %copy-start.5 = (f32[64,13]{0,1:T(8,128)S(1)}, f32[64,13]{0,1:T(8,128)}, u32[]{:S(2)}) copy-start(f32[64,13]{0,1:T(8,128)} %param.31) | copy-start | bytes 9988
  555.5 20.2 %copy-start.6 = (f32[64,13]{0,1:T(8,128)S(1)}, f32[64,13]{0,1:T(8,128)}, u32[]{:S(2)}) copy-start(f32[64,13]{0,1:T(8,128)} %param.36) | copy-start | bytes 9988

commit v4 on v3

--- a/solution.py
+++ b/solution.py
@@ -223,31 +223,17 @@
         for s in range(1, 8):
             hop = top_bit(s)
             src = own if s == hop else out.at[(s - hop) // 4, (s - hop) % 4]
-            dst = out.at[s // 4, s % 4]
-            parts = [slice(None)]
-            if s in (1, 3):
-                parts = [pl.ds(h * (D // 2), D // 2) for h in range(2)]
-            for h, cols in enumerate(parts):
-                self.ops[s, h] = net.add(
-                    lambda k, src=src, dst=dst, cols=cols, hop=hop: (
-                        src.at[:, cols], dst.at[:, cols], place.dev_t(hop),
-                    )
-                )
-
-    def named(self, which):
-        if isinstance(which, tuple):
-            return [self.ops[which]]
-        return [op for (s, _), op in self.ops.items() if s == which]
+            self.ops[s] = net.add(
+                lambda k, src=src, s=s, hop=hop: (src, out.at[s // 4, s % 4], place.dev_t(hop))
+            )
 
     def start(self, *which):
         for s in which:
-            for op in self.named(s):
-                op().start()
+            self.ops[s]().start()
 
     def wait(self, *which):
         for s in which:
-            for op in self.named(s):
-                op().wait_recv()
+            self.ops[s]().wait_recv()
 
 
 class GatherR:
@@ -406,7 +392,7 @@
     for part in to_r[0]:
         part.begin()
     start(to_t[1])
-    x_t.start(2)
+    x_t.start(2, 1)
     small_r.advance()
     for part in to_r[0]:
         part.advance()
@@ -424,9 +410,10 @@
 
     lax.fori_loop(0, 8, tables, 0)
     wait(to_t[1])
-    x_t.start(1)
     for part in to_r[1]:
         part.begin()
+    start(to_t[3])
+    start(to_t[2])
     small_r.end()
 
     smt[...] = sm[...].reshape(D, 128).T[:SMALLR, :]
@@ -582,15 +569,11 @@
                     lambda: [p.advance() for p in to_r[1]],
                     lambda: x_t.wait(2),
                     lambda: x_t.start(6),
-                    lambda: start(to_t[3]),
-                    lambda: start(to_t[2]),
                     lambda: x_t.wait(6),
                 ],
                 2: [
-                    lambda: x_t.wait((1, 0)),
-                    lambda: x_t.start((3, 0)),
-                    lambda: x_t.wait((1, 1)),
-                    lambda: x_t.start((3, 1), 5),
+                    lambda: x_t.wait(1),
+                    lambda: x_t.start(3, 5),
                     lambda: [p.end() for p in to_r[1]],
                     lambda: pltpu.make_async_copy(tu, ou, local.at[1]).start(),
                 ],
@@ -608,8 +591,7 @@
                     lambda: g_t.start(2),
                     lambda: x_t.wait(7),
                 ],
-                6: [lambda: g_t.wait((1, 0)), lambda: g_t.start((3, 0))],
-                7: [lambda: g_t.wait((1, 1)), lambda: g_t.start((3, 1), 5)],
+                7: [lambda: g_t.wait(1), lambda: g_t.start(3, 5)],
             },
         )
         late = k // 4
@@ -746,7 +728,7 @@
         pltpu.VMEM((8, FFT), F32),
         pltpu.VMEM((8, FFT), F32),
     ]
-    copies = 7 + 7 * 6 + (R - 1) * (1 + 8 + 2 * 8) + 18
+    copies = 7 + 7 * 6 + (R - 1) * (1 + 8 + 2 * 8) + 14
 
     def kernel(*refs):
         forward_kernel(n, lengths.shape[0], *refs)
@@ -1028,21 +1010,12 @@
     def __init__(self, net, place, data, cs, zs, ys, out):
         self.data, self.cs, self.zs, self.ys, self.out = data, cs, zs, ys, out
         self.hop_c = net.add(lambda k: (data.at[k], cs.at[k], place.dev_t(4)), 4)
-        self.near_z0 = net.add(lambda k: (cs.at[2], zs.at[0], place.dev_t(2)))
-        halves = [(slice(None), pl.ds(h * (D // 2), D // 2)) for h in range(2)]
-        self.halves = halves
-        self.far_z0 = [
-            net.add(lambda k, h=h: (cs.at[(3, *h)], zs.at[(1, *h)], place.dev_t(2)))
-            for h in halves
-        ]
-        self.hop_z1 = [
-            net.add(lambda k, h=h: (zs.at[(1, *h)], ys.at[(0, *h)], place.dev_t(1)))
-            for h in halves
-        ]
+        self.hop_z0 = net.add(lambda k: (cs.at[2 + k], zs.at[k], place.dev_t(2)), 2)
+        self.hop_z1 = net.add(lambda k: (zs.at[1], ys.at[0], place.dev_t(1)))
 
     @staticmethod
     def order(idx):
-        return 7 - 4 * (idx % 2) - 2 * (idx // 2 % 2) - idx // 4
+        return 7 - idx // 4 - 2 * (idx % 4)
 
     def loop(self, make, emit, after):
         def step(idx, carry):
@@ -1066,37 +1039,27 @@
                 self.hop_c(k).wait_recv()
                 emit(s, idx, near)
 
-                @pl.when(s == 3)
+                @pl.when(s >= 2)
                 def _():
-                    self.far_z0[0]().start()
-
-                @pl.when(s == 2)
-                def _():
-                    self.near_z0().start()
+                    self.hop_z0(s - 2).start()
 
             after(idx)
             return carry
 
         lax.fori_loop(0, 8, step, 0)
 
-    def more(self):
-        self.far_z0[1]().start()
-
-    def turn(self, h):
-        self.far_z0[h]().wait_recv()
-        mine, there = self.cs.at[(1, *self.halves[h])], self.zs.at[(1, *self.halves[h])]
-        add_rows(there, mine, there)
-        self.hop_z1[h]().start()
+    def turn_z1(self):
+        self.hop_z0(1).wait_recv()
+        add_rows(self.zs.at[1], self.cs.at[1], self.zs.at[1])
+        self.hop_z1().start()
 
     def turn_own(self):
-        self.near_z0().wait_recv()
+        self.hop_z0(0).wait_recv()
         add_rows(self.zs.at[0], self.cs.at[0], self.zs.at[0])
 
     def end(self):
-        for h in range(2):
-            self.hop_z1[h]().wait_recv()
-            where = self.halves[h]
-            add_rows(self.out.at[where], self.zs.at[(0, *where)], self.ys.at[(0, *where)])
+        self.hop_z1().wait_recv()
+        add_rows(self.out, self.zs.at[0], self.ys.at[0])
 
 
 def fold_scratch():
@@ -1223,9 +1186,13 @@
     keys = FoldR(net, place, lambda i: dk.at[i], kown, ks, both[0])
     values = FoldR(net, place, lambda i: dv.at[i], vown, vs, both[1])
     total = FoldT(net, place, data, cs, zs, ys, p_own)
-    up, pieces = half_fold(
-        net, place, g_up.reshape(4, n // 8, 2 * (D // n), FFT), 0, uown, us
-    )
+    ups, pieces = [], []
+    for h in range(2):
+        fold, near_pieces = half_fold(
+            net, place, g_up.reshape(4, n // 8, 2 * (D // n), FFT), h, uown.at[h], us.at[h]
+        )
+        ups.append(fold)
+        pieces += near_pieces
     keys.both().start()
     values.both().start()
 
@@ -1264,31 +1231,24 @@
     def after(idx):
         @pl.when(idx == 3)
         def _():
-            total.more()
             keys.first().start()
             values.first().start()
 
-        @pl.when(idx == 4)
-        def _():
-            total.turn(0)
-
-        @pl.when(idx == 5)
+        @pl.when(idx == 6)
         def _():
             for copy in loads[4:]:
                 copy.wait()
             keys.advance()
             values.advance()
 
-        @pl.when(idx == 6)
-        def _():
-            total.turn(1)
-
     total.loop(make, emit, after)
+    total.turn_z1()
     gradient_tiles(a2, tiles, turned, fetch_sem, [(dhv, st_wide, g_up, put_sem.at[0])])
     own_loads = [
         pltpu.make_async_copy(src, dst, near.at[k]) for k, (src, dst) in enumerate(pieces)
     ]
-    up.begin()
+    for up in ups:
+        up.begin()
     for copy in own_loads:
         copy.start()
     keys.gather()
@@ -1302,12 +1262,14 @@
     )
     for copy in own_loads:
         copy.wait()
-    up.advance()
+    for up in ups:
+        up.advance()
     keys.end(dk_own)
     values.end(dv_own)
     total.turn_own()
-    up.gather()
-    up.end(up_sum)
+    for h, up in enumerate(ups):
+        up.gather()
+        up.end(up_sum.at[h])
     total.end()
     net.finish()
 
@@ -1320,7 +1282,7 @@
         jax.ShapeDtypeStruct((TOK, D), F32),
         jax.ShapeDtypeStruct(head, BF),
         jax.ShapeDtypeStruct(head, BF),
-        jax.ShapeDtypeStruct(half, BF),
+        jax.ShapeDtypeStruct((2, *half), BF),
         jax.ShapeDtypeStruct((D, HEAD), BF),
         jax.ShapeDtypeStruct((D, FFT), BF),
         jax.ShapeDtypeStruct((D, FFT), BF),
@@ -1338,8 +1300,8 @@
         pltpu.VMEM((WIDE, 8 * TOK), BF),
         pltpu.VMEM((2, WIDE, FFT), BF),
         pltpu.VMEM((2, WIDE, HEAD), BF),
-        pltpu.VMEM((2, *half), BF),
-        pltpu.VMEM((3, *half), BF),
+        pltpu.VMEM((2, 2, *half), BF),
+        pltpu.VMEM((2, 3, *half), BF),
     ]
 
     def kernel(*refs):
@@ -1352,12 +1314,12 @@
         out_specs=[VM] * 4 + [ANY] * 3,
         scratch_shapes=[
             *scratch,
-            pltpu.SemaphoreType.DMA((18,)),
-            pltpu.SemaphoreType.DMA((18,)),
+            pltpu.SemaphoreType.DMA((19,)),
+            pltpu.SemaphoreType.DMA((19,)),
             pltpu.SemaphoreType.DMA((9,)),
             pltpu.SemaphoreType.DMA((2,)),
             pltpu.SemaphoreType.DMA((2, 2)),
-            pltpu.SemaphoreType.DMA((2,)),
+            pltpu.SemaphoreType.DMA((4,)),
         ],
         compiler_params=pltpu.CompilerParams(
             collective_id=2, has_side_effects=True, vmem_limit_bytes=62 * MIB
@@ -1366,10 +1328,10 @@
 
 
 def return_two_kernel(
-    n, gi, gu0, gu, go, gd, dq, dk, dv, a1, x, dh, w_in, w_up, cosine, sine, smt, stats, sums,
+    n, gi, gu, go, gd, dq, dk, dv, a1, x, dh, w_in, w_up, cosine, sine, smt, stats, sums,
     oi, ou, oo, od, e_own, osmall, gi_out,
     dqv, dkv, dvv, djp, djn, dhv, wi, wu, xt, cst, snt, data, cs, zs, ys,
-    uown, us, ui, uo, ud, si, so, sd, term, blocks, sslots, tiles, turned, st_in,
+    ui, uo, ud, si, so, sd, term, blocks, sslots, tiles, turned, st_in,
     send, recv, load, near, x_sem, fetch_sem, put_sem, last_sem,
 ):
     del gi
@@ -1389,7 +1351,6 @@
         net, place, lambda i: blocks.at[place.rr_of(i)], None, sslots, both[0]
     )
     total = FoldT(net, place, data, cs, zs, ys, e_own)
-    up, up_pieces = half_fold(net, place, gu.reshape(4, R, 2 * rb, FFT), 1, uown, us)
 
     finals = []
     ends = []
@@ -1402,7 +1363,7 @@
             )
         )
     for h in range(2):
-        summed = us.at[2] if h else gu0
+        summed = gu.at[h]
         ends.append(
             (
                 lambda zt, rows, cols, summed=summed: summed.at[zt, rows, cols],
@@ -1455,10 +1416,10 @@
             else:
                 op().wait_recv()
 
-    up.begin()
     for part in parts[0]:
         part.begin()
     send_finals(3)
+    send_finals(4)
     loads = [
         pltpu.make_async_copy(src, dst, load.at[k])
         for k, (src, dst) in enumerate(
@@ -1472,9 +1433,9 @@
         copy.start()
     own_loads = [
         pltpu.make_async_copy(src, dst, near.at[k])
-        for k, (src, dst) in enumerate(pieces + up_pieces)
+        for k, (src, dst) in enumerate(pieces)
     ]
-    for copy in own_loads[:8] + own_loads[12:]:
+    for copy in own_loads[:8]:
         copy.start()
 
     def fetch_x(s, slot):
@@ -1541,27 +1502,15 @@
         lax.fori_loop(0, D // chunk_cols, chunk, 0)
 
     def after(idx):
-        @pl.when(idx == 1)
-        def _():
-            for copy in own_loads[12:]:
-                copy.wait()
-            up.advance()
-
         @pl.when(idx == 2)
         def _():
-            total.more()
             for copy in own_loads[:4]:
                 copy.wait()
             for part in parts[0]:
                 part.advance()
-            up.gather()
-            up.end()
-            send_finals(4)
 
         @pl.when(idx == 3)
         def _():
-            total.turn(0)
-
             def rest(k, carry):
                 paired_joint(6 - 2 * k)
                 natural_joint(6 - 2 * k)
@@ -1573,7 +1522,7 @@
                 part.begin()
             for copy in own_loads[8:12]:
                 copy.start()
-            total.turn(1)
+            total.turn_z1()
             for part in parts[0]:
                 part.gather()
                 part.end()
@@ -1633,7 +1582,7 @@
     net.finish()
 
 
-def return_two(n, up_sum, g_up, g_out, g_down, dq, dk, dv, a1, x, dh, w_in, w_up, cosine, sine, smt, stats, sums):
+def return_two(n, up_sum, g_out, g_down, dq, dk, dv, a1, x, dh, w_in, w_up, cosine, sine, smt, stats, sums):
     rb = D // n
     R = n // 8
     head, cols, block = (8, TOK, HEAD), (8, TOK, FFT), (8, TOK, D)
@@ -1657,8 +1606,6 @@
         pltpu.VMEM((8, TOK, HEAD // 2), F32),
         pltpu.VMEM((8, TOK, HEAD // 2), F32),
         *fold_scratch(),
-        pltpu.VMEM((2, 4, 2 * rb, FFT // 2), BF),
-        pltpu.VMEM((3, 4, 2 * rb, FFT // 2), BF),
         *[pltpu.VMEM((2, 2, 2, 2 * rb, wide[k]), BF) for k in (0, 2, 3)],
         *[pltpu.VMEM((2, 3, 2, 2 * rb, wide[k]), BF) for k in (0, 2, 3)],
         pltpu.VMEM((SMALLR, D), F32),
@@ -1668,7 +1615,7 @@
         pltpu.VMEM((HEAD, 8 * TOK), BF),
         pltpu.VMEM((2, HEAD, 3 * HEAD), BF),
     ]
-    copies = 6 * 3 + 3 + 3 + 9 + 7 * 7 + 7
+    copies = 6 * 3 + 3 + 7 + 7 * 7 + 7
 
     def kernel(*refs):
         return_two_kernel(n, None, *refs)
@@ -1676,7 +1623,7 @@
     return pl.pallas_call(
         kernel,
         out_shape=outs,
-        in_specs=[ANY] * 14 + [VM] * 3,
+        in_specs=[ANY] * 13 + [VM] * 3,
         out_specs=[ANY] * 4 + [VM] + [ANY] * 2,
         scratch_shapes=[
             *scratch,
@@ -1692,7 +1639,7 @@
         compiler_params=pltpu.CompilerParams(
             collective_id=3, has_side_effects=True, vmem_limit_bytes=62 * MIB
         ),
-    )(up_sum, g_up, g_out, g_down, dq, dk, dv, a1, x, dh, w_in, w_up, cosine, sine, smt, stats, sums)
+    )(up_sum, g_out, g_down, dq, dk, dv, a1, x, dh, w_in, w_up, cosine, sine, smt, stats, sums)
 
 
 def token_row(base, core, size=RUN):
@@ -2102,11 +2049,11 @@
     o, dq = o4.reshape(8, TOK, HEAD), dq4.reshape(8, TOK, HEAD)
     dk, dv = dk5.reshape(R, 8, TOK, HEAD), dv5.reshape(R, 8, TOK, HEAD)
     if R == 4:
-        p_own, dk, dv, up_sum, g_out, g_down, g_up = return_one(
+        p_own, dk, dv, up_sum, g_out, g_down, _ = return_one(
             n, dk, dv, o, z, ws[2].reshape(D, -1), ws[3].reshape(D, -1), gg, a2, dh
         )
         *weight_grads, e_own, small_parts, _ = return_two(
-            n, up_sum, g_up, g_out, g_down, dq, dk, dv, a1, xg, dh,
+            n, up_sum, g_out, g_down, dq, dk, dv, a1, xg, dh,
             ws[0].reshape(D, -1), ws[1].reshape(D, -1), cosine, sine, small_all, stats_x, sums,
         )
         own_lanes = lax.dynamic_slice(

time: 579 us -> 567 us (0.979)
  Pallas kernels: 568 us -> 554 us
    pallas_call x1, Pallas kernels: 157 us -> 145 us  [return_two(): pl.pallas_call(kernel, out_shape=outs, in_specs=[ANY] * 13 + [VM] * 3, ou...]
where the time goes in v4:
time: 567 us; the launch traced here: 563 us
  Pallas kernels  554 us (98%)
  other arithmetic  6.36 us (1%)
    pallas_call x1, Pallas kernels, forward(): pl.pallas_call(kernel, out_shape=outs, in_specs=[ANY] * 7 + [pl.BlockSpec...  230 us
    pallas_call x1, Pallas kernels, return_two(): pl.pallas_call(kernel, out_shape=outs, in_specs=[ANY] * 13 + [VM] * 3, ou...  145 us
    pallas_call x1, Pallas kernels, return_one(): pl.pallas_call(kernel, out_shape=outs, in_specs=[ANY] * 9, out_specs=[VM]...  119 us
    pallas_call x1, Pallas kernels, attend_back(): pl.pallas_call(kernel, out_shape=[jax.ShapeDtypeStruct((2, 4, TOK, HEAD),...  22.6 us
    pallas_call x1, Pallas kernels, adam(): pl.pallas_call(kernel, out_shape=[*outs, *own_outs], grid=(steps,), in_sp...  20.1 us
    pallas_call x1, Pallas kernels, attend(): pl.pallas_call(kernel, out_shape=[jax.ShapeDtypeStruct((2, 4, TOK, HEAD),...  17.9 us

profile of v4, /device:TPU:0, one launch (start us, length us, event | category | flops | bytes accessed | tf_op | source)
XLA Modules:
  0.0 562.9 jit_solution(13300755827692023309)
XLA Ops:
  0.7 1.5 convert_element_type.14
  2.2 0.1 copy.37
  2.3 0.1 fusion.2
  2.4 0.2 fusion.3
  2.7 0.0 copy-start
  2.7 0.3 pad_maximum_fusion.1
  3.0 0.2 copy.38
  3.2 0.0 copy-start.1
  3.3 0.9 pad_maximum_fusion.refs_2_
  4.2 0.1 copy-done
  4.3 1.1 convert_element_type.15.refs_3_
  5.3 1.1 convert_element_type.17.refs_5_
  6.4 0.0 copy-done.2
  6.4 0.7 convert_element_type.16.refs_4_
  7.2 0.1 copy.36
  7.3 0.6 pad.4.refs_6_
  7.9 229.9 %shard_map.314 = (bf16[2,4,256,2048]{3,2,1,0:T(8,128)(2,1)}, bf16[2,4,256,2048]{3,2,1,0:T(8,128)(2,1)}, bf16[2,4,256,2048]{3,2,1,0:T(8,128)(2,1)}, bf16[2,4,256,...) custom-call(bf16[256,2048]{1,0:T(8,128)(2,1)} %refs_0_.7, ...), custom_call_target="tpu_custom_call" | custom-call | tf_op jit(solution)/shard_map/pallas_call | solution.py:736
  237.8 17.9 %shard_map.315 = (bf16[2,4,256,256]{3,2,1,0:T(8,128)(2,1)}, f32[4,8,512]{2,1,0:T(8,128)}) custom-call(s32[4]{0:T(128)} %refs_0_.6, bf16[2,4,256,256]{3,2,1,0:T(8,128)(2,1)} %get-tuple-element.67.refs_1_, bf16[2,4,256,256]{3,2,1,0:T(8,128)(2,1)} %get-tuple-element.68.refs_2_, bf16[4,2,4,256,256]{4,3,2,1,0:T(8,128)(2,1)} %get-tuple-element.69.refs_3_.refs_4_, ...), custom_call_target="tpu_custom_call" | custom-call | flops 4294967296 | bytes 12582912 | tf_op jit(solution)/shard_map/pallas_call | solution.py:1757
  255.7 22.6 %shard_map.316 = (f32[2,4,256,256]{3,2,1,0:T(8,128)}, bf16[4,2,4,256,256]{4,3,2,1,0:T(8,128)(2,1)}, bf16[4,2,4,256,256]{4,3,2,1,0:T(8,128)(2,1)}) custom-call(s32[4]{0:T(128)} %refs_0_.6, bf16[2,4,256,256]{3,2,1,0:T(8,128)(2,1)} %get-tuple-element.67.refs_1_, bf16[2,4,256,256]{3,2,1,0:T(8,128)(2,1)} %get-tuple-element.68.refs_2_, ...), custom_call_target="tpu_custom_call" | custom-call | flops 10737418240 | bytes 25165824 | tf_op jit(solution)/shard_map/pallas_call | solution.py:1849
  278.3 118.6 %shard_map.317 = (f32[256,2048]{1,0:T(8,128)}, bf16[8,256,256]{2,1,0:T(8,128)(2,1)}, bf16[8,256,256]{2,1,0:T(8,128)(2,1)}, bf16[2,4,128,512]{3,2,1,0:T(8,128)(2,...) custom-call(bf16[4,8,256,256]{3,2,1,0:T(8,128)(2,1)} %bitcast.40, ...), custom_call_target="tpu_custom_call" | custom-call | tf_op jit(solution)/shard_map/pallas_call | solution.py:1310
  396.9 145.1 %shard_map.318 = (bf16[64,6144]{1,0:T(8,128)(2,1)}, bf16[64,8192]{1,0:T(8,128)(2,1)}, bf16[64,2048]{1,0:T(8,128)(2,1)}, bf16[64,8192]{1,0:T(8,128)(2,1)}, f32[25...) custom-call(bf16[2,4,128,512]{3,2,1,0:T(8,128)(2,1)} %get-tuple-element.81.refs_0_, ...), custom_call_target="tpu_custom_call" | custom-call | tf_op jit(solution)/shard_map/pallas_call | solution.py:1623
  542.0 0.0 copy-start.5
  542.0 20.1 %shard_map.319 = (f32[64,6144]{1,0:T(8,128)}, f32[64,8192]{1,0:T(8,128)}, f32[64,2048]{1,0:T(8,128)}, f32[64,8192]{1,0:T(8,128)}, f32[64,6144]{1,0:T(8,128)}, /*...) custom-call(bf16[256,2048]{1,0:T(8,128)(2,1)} %refs_0_.7, ...), custom_call_target="tpu_custom_call" | custom-call | tf_op jit(solution)/shard_map/pallas_call | solution.py:1930
  562.2 0.7 multiply_subtract_fusion
  (12 shorter events, 0.1 us)
Async XLA Ops:
  2.7 1.6 copy-start
  3.2 2.1 copy-start.1
  5.3 1.1 copy-start.2
  5.3 1.8 copy-start.4
  542.0 20.1 %copy-start.3 = (f32[8,16,128]{2,1,0:T(8,128)S(1)}, f32[8,16,128]{2,1,0:T(8,128)}, u32[]{:S(2)}) copy-start(f32[8,16,128]{2,1,0:T(8,128)} %get-tuple-element.108) | copy-start | bytes 196612
  542.0 20.2 %copy-start.5 = (f32[64,13]{0,1:T(8,128)S(1)}, f32[64,13]{0,1:T(8,128)}, u32[]{:S(2)}) copy-start(f32[64,13]{0,1:T(8,128)} %param.31) | copy-start | bytes 9988
  542.0 20.2 %copy-start.6 = (f32[64,13]{0,1:T(8,128)S(1)}, f32[64,13]{0,1:T(8,128)}, u32[]{:S(2)}) copy-start(f32[64,13]{0,1:T(8,128)} %param.36) | copy-start | bytes 9988
